TPU v7x, 256 devices: a whole 4x4x8 slice. The times are simulated.
256 devices in a mesh: dp: 64 (over z, y, core), mp: 4 (over x).
Axes of the slice: x: 4, y: 4, z: 8, core: 2. Of those that a mesh axis runs over, the one named last changes fastest.
Arguments:
- texts: bfloat16 [1536, 128, 1024], P('dp')
- w_qkv: bfloat16 [1024, 3072], P(None, 'mp'), may hold values from -0.1875 to 0.1875
- w_out: bfloat16 [1024, 1024], P('mp'), may hold values from -0.75 to 0.75
- w_self: bfloat16 [1024, 1024], P('mp'), may hold values from -0.1875 to 0.1875
- w_neigh: bfloat16 [1024, 1024], P('mp'), may hold values from -0.1875 to 0.1875
- neighbours: int32 [1536, 16], P('dp'), may hold values from -1 to 1535, as said below
- cotangent: bfloat16 [1536, 1024], P('dp', 'mp'), may hold values from -6 to 6
Outputs:
- mixed: bfloat16 [1536, 1024], P('dp', 'mp')
- node_grad: bfloat16 [1536, 1024], P('dp', 'mp')
- grad_w_self: float32 [1024, 1024], P('mp')
- grad_w_neigh: float32 [1024, 1024], P('mp')
- grad_w_out: float32 [1024, 1024], P('mp')
Inputs may be any that keep to these rules, and one draw needn't show every extreme that they name: `neighbours`: A node id j lives with index j // 24 of dp. In the rows of one dp device (aligned blocks of 24 rows) at most 6 entries fall in any one owner's id range, and some owner gets exactly 6; entries are -1 or ids below 1536. Some targets have every slot -1.
All inputs are finite; a program needn't handle non-finite values.
Results may differ from a plain program's by a relative error of at most 0.029.
The roundings to bfloat16 on the way count: a program that leaves them out, or rounds other values in their place, can miss the bound.
Values may be sent and summed in bfloat16 or wider, within the bound.
A program may use at most 64 MiB of HBM per device.

v0:
```python
import jax
import jax.numpy as jnp
from jax import lax
from jax.sharding import PartitionSpec as P

HD = 64


def per_device(texts, w_qkv, w_out, w_self, w_neigh, neighbours, cotangent):
    node_dev, seq_len, width = texts.shape
    fan = neighbours.shape[1]
    cols = w_self.shape[0]
    heads_here = w_qkv.shape[1] // (3 * HD)
    groups = lax.axis_size("dp")
    slots = node_dev * fan
    limit = slots // groups
    factor = 1.0 / jnp.sqrt(jnp.float32(node_dev * groups))
    qkv = jnp.einsum("nld,de->nle", texts, w_qkv, preferred_element_type=jnp.float32).astype(
        jnp.bfloat16
    )
    qkv = qkv.reshape(node_dev, seq_len, heads_here, 3, HD)
    scores = jnp.einsum(
        "nqhd,nkhd->nhqk",
        qkv[:, :, :, 0, :],
        qkv[:, :, :, 1, :],
        preferred_element_type=jnp.float32,
    )
    probs = jax.nn.softmax(scores / jnp.sqrt(jnp.float32(HD)), axis=-1).astype(jnp.bfloat16)
    context = jnp.einsum(
        "nhqk,nkhd->nhd", probs, qkv[:, :, :, 2, :], preferred_element_type=jnp.float32
    )
    pooled = (
        (context / jnp.float32(seq_len)).reshape(node_dev, heads_here * HD).astype(jnp.bfloat16)
    )
    partial_embed = jnp.dot(pooled, w_out, preferred_element_type=jnp.float32)
    token_mean = jnp.mean(texts.astype(jnp.float32), axis=1)
    embed = (token_mean + lax.psum(partial_embed, "mp")).astype(jnp.bfloat16)
    start_col = lax.axis_index("mp") * cols
    embed_cols = lax.dynamic_slice_in_dim(embed, start_col, cols, 1)
    valid = neighbours >= 0
    cnt = jnp.maximum(jnp.sum(valid, axis=1).astype(jnp.float32), 1.0)
    flat_ids = neighbours.reshape(slots)
    flat_valid = flat_ids >= 0
    owner = jnp.where(flat_valid, flat_ids // node_dev, 0)
    local = jnp.where(flat_valid, flat_ids % node_dev, 0)
    owner_hot = ((owner[:, None] == jnp.arange(groups)[None, :]) & flat_valid[:, None]).astype(
        jnp.int32
    )
    before = jnp.cumsum(owner_hot, axis=0) - owner_hot
    rank = jnp.sum(before * owner_hot, axis=1)
    position = jnp.where(flat_valid, owner * limit + rank, slots)
    wanted = (
        jnp.full((slots,), -1, jnp.int32)
        .at[position]
        .set(local, mode="drop")
        .reshape(groups, limit)
    )
    asked = lax.all_to_all(wanted, "dp", split_axis=0, concat_axis=0, tiled=True).reshape(slots)
    select = (asked[:, None] == jnp.arange(node_dev)[None, :]).astype(jnp.bfloat16)
    sending = jnp.dot(select, embed_cols, preferred_element_type=jnp.float32).astype(jnp.bfloat16)
    arrived = lax.all_to_all(
        sending.reshape(groups, limit, cols), "dp", split_axis=0, concat_axis=0, tiled=True
    ).reshape(slots, cols)
    gather_hot = jnp.sum(
        position.reshape(node_dev, fan)[:, :, None] == jnp.arange(slots)[None, None, :], axis=1
    ).astype(jnp.bfloat16)
    agg = (jnp.dot(gather_hot, arrived, preferred_element_type=jnp.float32) / cnt[:, None]).astype(
        jnp.bfloat16
    )
    partial_z = jnp.dot(embed_cols, w_self, preferred_element_type=jnp.float32) + jnp.dot(
        agg, w_neigh, preferred_element_type=jnp.float32
    )
    z_cols = lax.psum_scatter(partial_z, "mp", scatter_dimension=1, tiled=True)
    mixed = jax.nn.gelu(z_cols).astype(jnp.bfloat16)
    _, pullback = jax.vjp(jax.nn.gelu, z_cols)
    dz_cols = pullback(cotangent.astype(jnp.float32))[0].astype(jnp.bfloat16)
    dz_full = lax.all_gather(dz_cols, "mp", axis=1, tiled=True)
    d_agg = lax.dot_general(
        dz_full, w_neigh, (((1,), (1,)), ((), ())), preferred_element_type=jnp.float32
    )
    msg = (d_agg / cnt[:, None]).astype(jnp.bfloat16)
    self_term = lax.dot_general(
        dz_full, w_self, (((1,), (1,)), ((), ())), preferred_element_type=jnp.float32
    )
    slot_msgs = lax.dot_general(
        gather_hot, msg, (((0,), (0,)), ((), ())), preferred_element_type=jnp.float32
    ).astype(jnp.bfloat16)
    returned = lax.all_to_all(
        slot_msgs.reshape(groups, limit, cols), "dp", split_axis=0, concat_axis=0, tiled=True
    ).reshape(slots, cols)
    neighbour_sum = lax.dot_general(
        select, returned, (((0,), (0,)), ((), ())), preferred_element_type=jnp.float32
    )
    node_grad = (self_term + neighbour_sum).astype(jnp.bfloat16)
    grad_full = lax.all_gather(node_grad, "mp", axis=1, tiled=True)
    local_self = lax.dot_general(
        embed_cols, dz_full, (((0,), (0,)), ((), ())), preferred_element_type=jnp.float32
    )
    local_neigh = lax.dot_general(
        agg, dz_full, (((0,), (0,)), ((), ())), preferred_element_type=jnp.float32
    )
    local_out = lax.dot_general(
        pooled, grad_full, (((0,), (0,)), ((), ())), preferred_element_type=jnp.float32
    )
    sum_self, sum_neigh, sum_out = lax.psum((local_self, local_neigh, local_out), "dp")
    return (mixed, node_grad, sum_self * factor, sum_neigh * factor, sum_out * factor)


def solution(mesh):
    return jax.shard_map(
        per_device,
        mesh=mesh,
        in_specs=(
            P("dp", None, None),
            P(None, "mp"),
            P("mp", None),
            P("mp", None),
            P("mp", None),
            P("dp", None),
            P("dp", "mp"),
        ),
        out_specs=(P("dp", "mp"), P("dp", "mp"), P("mp", None), P("mp", None), P("mp", None)),
        check_vma=False,
    )
```

profile of v0, /device:TPU:1, one launch (start us, length us, event | category | flops | bytes accessed | tf_op | source)
XLA Modules:
  0.0 385.3 jit_solution(15571976316331499537)
XLA Ops:
  7.2 1.4 copy-done
  8.6 9.5 %convolution_convert_fusion = bf16[24,128,768]{2,1,0:T(8,128)(2,1)} fusion(bf16[24,128,1024]{2,1,0:T(8,128)(2,1)} %param.7, bf16[1024,768]{1,0:T(8,128)(2,1)S(1)} %copy-done), kind=kOutput, calls=%fused_computation.10 | convolution fusion | flops 4834197504 | bytes 12582912 | tf_op jit(solution)/shard_map/nld,de->nle/dot_general | solution.py:18
  18.0 6.7 %copy.32 = bf16[24,128,768]{1,2,0:T(8,128)(2,1)} copy(bf16[24,128,768]{2,1,0:T(8,128)(2,1)} %convolution_convert_fusion) | data formatting | bytes 9437184 | tf_op jit(solution)/shard_map/convert_element_type | solution.py:18
  24.7 5.6 %fusion.7 = f32[24,4,128,128]{2,3,1,0:T(8,128)} fusion(bf16[24,128,4,3,64]{1,4,3,2,0:T(8,128)(2,1)} %bitcast.64), kind=kOutput, calls=%fused_computation.14 | convolution fusion | flops 201326592 | bytes 9437184 | tf_op jit(solution)/shard_map/nqhd,nkhd->nhqk/dot_general | solution.py:22
  30.4 6.8 %convert_reduce_fusion.1 = f32[24,4,128]{2,1,0:T(4,128)S(1)} fusion(f32[24,4,128,128]{2,3,1,0:T(8,128)} %fusion.7), kind=kOutput, calls=%fused_computation.4 | output fusion | flops 11022590 | bytes 6340608 | tf_op jit(solution)/shard_map/div | solution.py:28
  37.2 2.4 fusion.6
  43.1 2.9 scatter_custom_fusion
  46.8 13.2 %all-to-all-start = ((s32[64,1,6]{2,1,0:T(1,128)}), s32[64,1,6]{2,1,0:T(1,128)S(1)}, u32[]{:S(2)}, u32[]{:S(2)}) async-start(s32[64,1,6]{2,1,0:T(1,128)} %bitcast.10), calls=%async_computation | async-start | bytes 65536 | tf_op jit(solution)/shard_map/all_to_all | solution.py:58
  59.9 4.3 %convert_reduce_fusion = f32[24,1024]{1,0:T(8,128)S(1)} fusion(bf16[24,128,1024]{2,1,0:T(8,128)(2,1)} %param.7), kind=kLoop, calls=%fused_computation.3 | loop fusion | flops 6266880 | bytes 6389760 | tf_op jit(solution)/shard_map/reduce_sum | solution.py:36
  64.4 4.8 %all-to-all-done = s32[64,1,6]{2,1,0:T(1,128)S(1)} async-done(((s32[64,1,6]{2,1,0:T(1,128)}), s32[64,1,6]{2,1,0:T(1,128)S(1)}, u32[]{:S(2)}, u32[]{:S(2)}) %all-to-all-start) | async-done | bytes 1568 | tf_op jit(solution)/shard_map/all_to_all | solution.py:58
  70.6 18.0 %all-reduce.4.cloned.1.call-done = f32[24,1024]{1,0:T(8,128)} async-done(((f32[24,1024]{1,0:T(8,128)}), f32[24,1024]{1,0:T(8,128)}) %all-reduce.4.cloned.1.call-update) | async-done | bytes 98320 | tf_op jit(solution)/shard_map/psum | solution.py:37
  90.4 12.7 %all-to-all-start.1 = ((bf16[64,6,256]{2,1,0:T(8,128)(2,1)}), bf16[64,6,256]{2,1,0:T(8,128)(2,1)S(1)}, u32[]{:S(2)}, u32[]{:S(2)}) async-start(bf16[64,6,256]{2,1,0:T(8,128)(2,1)} %reshape.207), calls=%async_computation.1 | async-start | bytes 524288 | tf_op jit(solution)/shard_map/all_to_all | solution.py:61
  103.6 12.7 %all-to-all-done.1 = bf16[64,6,256]{2,1,0:T(8,128)(2,1)S(1)} async-done(((bf16[64,6,256]{2,1,0:T(8,128)(2,1)}), bf16[64,6,256]{2,1,0:T(8,128)(2,1)S(1)}, u32[]{:S(2)}, u32[]{:S(2)}) %all-to-all-start.1) | async-done | bytes 196640 | tf_op jit(solution)/shard_map/all_to_all | solution.py:61
  117.4 15.3 %reduce-scatter.2.cloned.1.call-done = f32[24,256]{1,0:T(8,128)} async-done(((f32[24,1024]{1,0:T(8,128)}), f32[24,256]{1,0:T(8,128)}) %reduce-scatter.2.cloned.1.call-update) | async-done | bytes 24592 | tf_op jit(solution)/shard_map/reduce_scatter | solution.py:73
  132.7 1.4 fusion.22
  134.1 9.0 %all_gather.6 = bf16[24,1024]{1,0:T(8,128)(2,1)S(1)} all-gather(bf16[24,256]{1,0:T(8,128)(2,1)S(1)} %get-tuple-element.12), channel_id=1, replica_groups=mesh['dp'=64,'mp'=4] {'mp'}, dimensions={1}, use_global_device_ids=true | all-gather | bytes 61440 | tf_op jit(solution)/shard_map/all_gather | solution.py:77
  143.6 1.3 fusion.51
  145.7 15.8 %all-to-all-start.2 = ((bf16[64,6,256]{2,1,0:T(8,128)(2,1)}), bf16[64,6,256]{2,1,0:T(8,128)(2,1)S(1)}, u32[]{:S(2)}, u32[]{:S(2)}) async-start(bf16[64,6,256]{2,1,0:T(8,128)(2,1)} %reshape.209), calls=%async_computation.3 | async-start | bytes 524288 | tf_op jit(solution)/shard_map/all_to_all | solution.py:88
  161.8 1.3 fusion.52
  163.1 11.6 %all-to-all-done.2 = bf16[64,6,256]{2,1,0:T(8,128)(2,1)S(1)} async-done(((bf16[64,6,256]{2,1,0:T(8,128)(2,1)}), bf16[64,6,256]{2,1,0:T(8,128)(2,1)S(1)}, u32[]{:S(2)}, u32[]{:S(2)}) %all-to-all-start.2) | async-done | bytes 196640 | tf_op jit(solution)/shard_map/all_to_all | solution.py:88
  175.1 9.0 %all_gather.7 = bf16[24,1024]{1,0:T(8,128)(2,1)S(1)} all-gather(bf16[24,256]{1,0:T(8,128)(2,1)S(1)} %fusion.10), channel_id=1, replica_groups=mesh['dp'=64,'mp'=4] {'mp'}, dimensions={1}, use_global_device_ids=true | all-gather | bytes 61440 | tf_op jit(solution)/shard_map/all_gather | solution.py:95
  185.4 187.7 %all-reduce.6.cloned.1.call-done = (f32[256,1024]{1,0:T(8,128)}, f32[256,1024]{1,0:T(8,128)}, f32[256,1024]{1,0:T(8,128)}) async-done(((f32[256,1024]{1,0:T(8,128)}, f32[256,1024]{1,0:T(8,128)}, f32[256,1024]{1,0:T(8,128)}), (f32[256,1024]{1,0:T(8,128)}, f32[256,1024]{1,0:T(8,128)}, f32[256,1024]{1,0:T(8,128)})) %all-reduce.6.cloned.1.call-update) | async-done | bytes 3145744 | tf_op jit(solution)/shard_map/psum | solution.py:105
  373.2 2.3 broadcast_multiply_fusion.2
  375.5 3.2 broadcast_multiply_fusion
  (64 shorter events, 12.2 us)
Async XLA Ops:
  7.2 1.4 copy-start
  7.2 81.5 %all-reduce.4.cloned.1.call-start = ((), (), s32[]{:S(2)}) async-start(), calls=%async_computation.4 | async-start | bytes 196608 | tf_op jit(solution)/shard_map/psum | solution.py:37
  30.4 9.4 %copy-start.3 = (bf16[256,1024]{1,0:T(8,128)(2,1)S(1)}, bf16[256,1024]{1,0:T(8,128)(2,1)}, u32[]{:S(2)}) copy-start(bf16[256,1024]{1,0:T(8,128)(2,1)} %param.9) | copy-start | bytes 1572868
  30.4 10.3 %copy-start.6 = (s32[24,16]{0,1:T(8,128)S(1)}, s32[24,16]{0,1:T(8,128)}, u32[]{:S(2)}) copy-start(s32[24,16]{0,1:T(8,128)} %param.12) | copy-start | bytes 4612
  37.2 66.3 %copy-start.1 = (bf16[256,1024]{1,0:T(8,128)(2,1)S(1)}, bf16[256,1024]{1,0:T(8,128)(2,1)}, u32[]{:S(2)}) copy-start(bf16[256,1024]{1,0:T(8,128)(2,1)} %param.10) | copy-start | bytes 1572868
  37.2 79.4 %copy-start.2 = (bf16[256,1024]{1,0:T(8,128)(2,1)S(1)}, bf16[256,1024]{1,0:T(8,128)(2,1)}, u32[]{:S(2)}) copy-start(bf16[256,1024]{1,0:T(8,128)(2,1)} %param.11) | copy-start | bytes 1572868
  37.2 95.5 %copy-start.5 = (bf16[24,256]{1,0:T(8,128)(2,1)S(1)}, bf16[24,256]{1,0:T(8,128)(2,1)}, u32[]{:S(2)}) copy-start(bf16[24,256]{1,0:T(8,128)(2,1)} %param.13) | copy-start | bytes 36868
  46.8 22.5 %all-to-all-start = ((s32[64,1,6]{2,1,0:T(1,128)}), s32[64,1,6]{2,1,0:T(1,128)S(1)}, u32[]{:S(2)}, u32[]{:S(2)}) async-start(s32[64,1,6]{2,1,0:T(1,128)} %bitcast.10), calls=%async_computation | async-start | bytes 65536 | tf_op jit(solution)/shard_map/all_to_all | solution.py:58
  90.4 25.9 %all-to-all-start.1 = ((bf16[64,6,256]{2,1,0:T(8,128)(2,1)}), bf16[64,6,256]{2,1,0:T(8,128)(2,1)S(1)}, u32[]{:S(2)}, u32[]{:S(2)}) async-start(bf16[64,6,256]{2,1,0:T(8,128)(2,1)} %reshape.207), calls=%async_computation.1 | async-start | bytes 524288 | tf_op jit(solution)/shard_map/all_to_all | solution.py:61
  103.2 29.5 %reduce-scatter.2.cloned.1.call-start = ((), (), s32[]{:S(2)}) async-start(), calls=%async_computation.5 | async-start | bytes 122880 | tf_op jit(solution)/shard_map/reduce_scatter | solution.py:73
  145.7 29.0 %all-to-all-start.2 = ((bf16[64,6,256]{2,1,0:T(8,128)(2,1)}), bf16[64,6,256]{2,1,0:T(8,128)(2,1)S(1)}, u32[]{:S(2)}, u32[]{:S(2)}) async-start(bf16[64,6,256]{2,1,0:T(8,128)(2,1)} %reshape.209), calls=%async_computation.3 | async-start | bytes 524288 | tf_op jit(solution)/shard_map/all_to_all | solution.py:88
  161.5 211.6 %all-reduce.6.cloned.1.call-start = ((), (), s32[]{:S(2)}) async-start(), calls=%async_computation.6 | async-start | bytes 6291456 | tf_op jit(solution)/shard_map/psum | solution.py:105
  175.1 203.7 %copy-start.4 = (bf16[24,256]{1,0:T(8,128)(2,1)}, bf16[24,256]{1,0:T(8,128)(2,1)S(1)}, u32[]{:S(2)}) copy-start(bf16[24,256]{1,0:T(8,128)(2,1)S(1)} %fusion.10) | copy-start | bytes 36868
Sparse Core Ops, SparseCore 0:
  40.7 47.8 all-reduce.3
  117.5 15.1 reduce-scatter.1
  185.6 187.5 all-reduce.5
where the time goes:
time: 387 us; the launch traced here: 385 us
  waiting for transfers between devices  250 us (65%)
  starting transfers between devices  41.8 us (11%)
  matrix products  24.7 us (6%)
  other arithmetic  21.1 us (5%)
  blocking collectives  18 us (5%)
  local copies, waits for them, and re-layouts  15.4 us (4%)
  between operations  14 us (4%)
    psum x1, waiting for transfers between devices, per_device(): lax.psum((local_self, local_neigh, local_out), 'dp')  188 us
    psum x1, waiting for transfers between devices, per_device(): embed = (token_mean + lax.psum(partial_embed, 'mp')).astype(jnp.bfloat16)  18 us
    all_to_all x1, starting transfers between devices, per_device(): lax.all_to_all(slot_msgs.reshape(groups, limit, cols), 'dp', split_axis=0...  15.8 us
    reduce_scatter x1, waiting for transfers between devices, per_device(): z_cols = lax.psum_scatter(partial_z, 'mp', scatter_dimension=1, tiled=True)  15.3 us
    all_to_all x1, starting transfers between devices, per_device(): lax.all_to_all(wanted, 'dp', split_axis=0, concat_axis=0, tiled=True)  13.2 us
    all_to_all x1, starting transfers between devices, per_device(): lax.all_to_all(sending.reshape(groups, limit, cols), 'dp', split_axis=0,...  12.7 us
    all_to_all x1, waiting for transfers between devices, per_device(): lax.all_to_all(sending.reshape(groups, limit, cols), 'dp', split_axis=0,...  12.7 us
    all_to_all x1, waiting for transfers between devices, per_device(): lax.all_to_all(slot_msgs.reshape(groups, limit, cols), 'dp', split_axis=0...  11.6 us
  transfers between devices with their start and end apart: 6, of which 6 were waited for; matrix products, arithmetic and copies ran while one was open for 3% of the time, Pallas kernels for 0%

commit v1 on v0

v1 whole, which is shorter than its diff:
```python
import math

import jax
import jax.numpy as jnp
from jax import lax
from jax.experimental import pallas as pl
from jax.experimental.pallas import tpu as pltpu
from jax.sharding import PartitionSpec as P

MESH = pl.DeviceIdType.MESH
F32, BF16 = jnp.float32, jnp.bfloat16
HD = 64
NODE = 24
PAD = 32
DP, MP, NZ, NG, NY = 64, 4, 8, 8, 4
COLS, WIDTH = 256, 1024
SLOT = 16
EMPTY = 120.0
TEXTS = 2


def dot(a, b):
    return jnp.dot(a, b, preferred_element_type=F32)


def dot_nt(a, b):
    return lax.dot_general(a, b, (((1,), (1,)), ((), ())), preferred_element_type=F32)


def dot_tn(a, b):
    return lax.dot_general(a, b, (((0,), (0,)), ((), ())), preferred_element_type=F32)


def iota(shape, dim):
    return lax.broadcasted_iota(jnp.int32, shape, dim)


def pad_rows(x, rows):
    return jnp.concatenate([x, jnp.zeros((rows - x.shape[0], x.shape[1]), x.dtype)], axis=0)


def routing(nb_ref, want_ref, gh_ref, ght_ref, cnt_ref):
    nb = nb_ref[...]
    ids = nb.astype(F32)
    own = jnp.floor((ids + 0.5) * (1.0 / NODE))
    loc = ids - NODE * own
    live = nb >= 0
    cnt = jnp.maximum(jnp.sum(live.astype(F32), axis=1, keepdims=True), 1.0)
    cnt_ref[...] = jnp.concatenate(
        [jnp.broadcast_to(cnt, (NODE, COLS)), jnp.ones((PAD - NODE, COLS), F32)], axis=0
    )
    fan = nb.shape[1]
    groups = iota((NODE, DP), 1).astype(F32)
    hots = [(own[:, f : f + 1] == groups).astype(F32) for f in range(fan)]
    total = hots[0]
    for f in range(1, fan):
        total = total + hots[f]
    lower = (iota((NODE, NODE), 1) < iota((NODE, NODE), 0)).astype(BF16)
    run = dot(lower, total.astype(BF16))
    spots = iota((NODE, DP * SLOT), 1).astype(F32)
    left = jnp.zeros((NODE, DP * SLOT), F32)
    right = jnp.zeros((NODE, DP * SLOT), F32)
    names = jnp.zeros((NODE, DP * SLOT), F32)
    for f in range(fan):
        rank = jnp.sum(hots[f] * run, axis=1, keepdims=True)
        run = run + hots[f]
        at = jnp.where(live[:, f : f + 1], own[:, f : f + 1] * SLOT + rank, -1000.0)
        name = loc[:, f : f + 1]
        is_left = spots == at
        is_right = spots == at + 8.0
        left = left + is_left.astype(F32)
        right = right + is_right.astype(F32)
        names = names + jnp.where(is_left, name - EMPTY, 0.0)
        names = names + jnp.where(is_right, name + (PAD - EMPTY), 0.0)
    gap = jnp.zeros((PAD - NODE, DP * SLOT), F32)
    both = jnp.concatenate([left, gap, right, gap], axis=0)
    gh_ref[...] = both.astype(BF16)
    ght_ref[...] = jnp.transpose(pad_rows(both, 128)).astype(BF16)
    spread = jnp.transpose(pad_rows(names, 128)).astype(BF16)
    want_ref[...] = (dot(spread, jnp.ones((128, 128), BF16)) + EMPTY).astype(BF16)


def attention_kernel(tx_ref, w_ref, nb_ref, pooled_ref, tmean_ref, want_ref, gh_ref, ght_ref, cnt_ref, wp, acc, tacc):
    step = pl.program_id(0)
    low = iota((1, 128), 1) < HD

    @pl.when(step == 0)
    def _():
        for pair in range(2):
            base = pair * 384
            a = w_ref[:, base : base + 128].astype(F32)
            b = w_ref[:, base + 128 : base + 256].astype(F32)
            c = w_ref[:, base + 256 : base + 384].astype(F32)
            wp[:, pair * 128 : pair * 128 + 128] = jnp.where(low, a, b).astype(BF16)
            wp[:, 256 + pair * 128 : 384 + pair * 128] = pltpu.roll(jnp.where(low, c, a), HD, 1).astype(BF16)
            wp[:, 512 + pair * 128 : 640 + pair * 128] = jnp.where(low, b, c).astype(BF16)
        routing(nb_ref, want_ref, gh_ref, ght_ref, cnt_ref)

    rows = TEXTS * 128
    x = tx_ref[...].reshape(rows, WIDTH)
    q = dot(x, wp[:, 0:256]).astype(BF16)
    k = dot(x, wp[:, 256:512]).astype(BF16)
    v = dot(x, wp[:, 512:768]).astype(BF16).astype(F32)
    ones = ((iota((256, 128), 0) < 128) == (iota((256, 128), 1) < HD)).astype(BF16)
    scale = 1.0 / (math.sqrt(HD) * math.log(2.0))
    zero = jnp.zeros((), BF16)
    for t in range(TEXTS):
        parts = []
        for pair in range(2):
            cols = slice(pair * 128, pair * 128 + 128)
            qt = q[t * 128 : t * 128 + 128, cols]
            kt = k[t * 128 : t * 128 + 128, cols]
            vt = v[t * 128 : t * 128 + 128, cols]
            two = jnp.concatenate([jnp.where(low, qt, zero), jnp.where(low, zero, qt)], axis=0)
            s = dot_nt(kt, two)
            e = jnp.exp2((s - jnp.max(s, axis=0, keepdims=True)) * scale)
            p = (e / jnp.sum(e, axis=0, keepdims=True)).astype(BF16)
            parts.append(jnp.sum(dot(p, ones) * vt, axis=0, keepdims=True) * (1.0 / 128))
        row = jnp.concatenate(parts, axis=1)
        acc[pl.ds(step * TEXTS + t, 1), :] = row
        mine = tx_ref[t, :, pl.ds(pl.multiple_of(lax.axis_index("mp") * COLS, COLS), COLS)]
        tacc[pl.ds(step * TEXTS + t, 1), :] = jnp.sum(mine.astype(F32), axis=0, keepdims=True) * (1.0 / 128)

    @pl.when(step == pl.num_programs(0) - 1)
    def _():
        pooled_ref[...] = pad_rows(acc[...], PAD).astype(BF16)
        tmean_ref[...] = tacc[...]


def attention(texts, w_qkv, neighbours):
    steps = NODE // TEXTS
    whole = lambda *shape: pl.BlockSpec(shape, lambda i: (0,) * len(shape))
    return pl.pallas_call(
        attention_kernel,
        grid=(steps,),
        out_shape=[
            jax.ShapeDtypeStruct((PAD, COLS), BF16),
            jax.ShapeDtypeStruct((NODE, COLS), F32),
            jax.ShapeDtypeStruct((DP * SLOT, 128), BF16),
            jax.ShapeDtypeStruct((2 * PAD, DP * SLOT), BF16),
            jax.ShapeDtypeStruct((DP * SLOT, 128), BF16),
            jax.ShapeDtypeStruct((PAD, COLS), F32),
        ],
        in_specs=[
            pl.BlockSpec((TEXTS, 128, WIDTH), lambda i: (i, 0, 0)),
            whole(WIDTH, 768),
            whole(NODE, 16),
        ],
        out_specs=[
            whole(PAD, COLS),
            whole(NODE, COLS),
            whole(DP * SLOT, 128),
            whole(2 * PAD, DP * SLOT),
            whole(DP * SLOT, 128),
            whole(PAD, COLS),
        ],
        scratch_shapes=[
            pltpu.VMEM((WIDTH, 768), BF16),
            pltpu.VMEM((NODE, COLS), F32),
            pltpu.VMEM((NODE, COLS), F32),
        ],
        compiler_params=pltpu.CompilerParams(
            dimension_semantics=("arbitrary",), vmem_limit_bytes=40 * 2**20
        ),
        cost_estimate=pl.CostEstimate(flops=6 * 10**9, bytes_accessed=9 * 10**6, transcendentals=1600000),
    )(texts, w_qkv, neighbours)


ASK, POOL_SUM, ROWS, EMB_G, POOL_G, AGG_G, Z_SUM, DZ, DZ_G, BACK, NG_G, SN_RS, SN_AG, OUT_RS, OUT_AG = range(15)


def graph_kernel(
    pooled, tmean, want, gh, ght, cnt, w_out, w_self, w_neigh, cot,
    mixed, ngrad, o_self, o_neigh, o_out,
    asked, sbuf, rbuf, sbuf2, rbuf2, sel_t, part, sums, zpart, zsums, e2, m2,
    emb_g, pool_g, agg_g, dzf, dz2, dz_g, ng2, ng_g, sn_s, sn_r, fin_sn, out_s, out_r, fin_out,
    ssem, rsem, y_s, y_r, c_s, c_r,
):
    m, d = lax.axis_index("mp"), lax.axis_index("dp")
    z, g = d // NG, d % NG
    y, c = g // 2, g % 2
    is_diag = (g // 2) == m

    def send(src, dst, phase, dp, mp):
        pltpu.make_async_remote_copy(
            src_ref=src, dst_ref=dst, send_sem=ssem.at[phase], recv_sem=rsem.at[phase],
            device_id=(dp, mp), device_id_type=MESH,
        ).start()

    def got(ref, phase):
        pltpu.make_async_copy(ref, ref, rsem.at[phase]).wait()

    def sent(ref, phase):
        pltpu.make_async_copy(ref, ref, ssem.at[phase]).wait()

    def over(count, body):
        def step(i, carry):
            body(i)
            return carry

        lax.fori_loop(1, count, step, 0)

    def to_dp(src, dst, phase):
        def one(i):
            to = (d + i) % DP
            send(src.at[to], dst.at[d], phase, to, m)

        over(DP, one)
        dst[d] = src[d]

    def to_mp(src, dst, phase):
        for i in range(1, MP):
            to = (m + i) % MP
            send(src.at[to], dst.at[m], phase, d, to)
        dst[m] = src[m]

    def to_group(block, phase):
        for i in range(1, NG):
            send(block.at[g], block.at[g], phase, z * NG + (g + i) % NG, m)

    def to_columns(src, dst, phase):
        def one(i, carry):
            mp, half = i // 2, i % 2
            at = 2 * m + half
            here = jnp.logical_and(mp == m, at == g)

            @pl.when(jnp.logical_not(here))
            def _():
                send(src.at[half], dst.at[g], phase, z * NG + at, mp)

            @pl.when(here)
            def _():
                dst[g] = src[half]

            return carry

        lax.fori_loop(0, 2 * MP, one, 0)

    def got_columns(dst, phase):
        @pl.when(is_diag)
        def _():
            got(dst.at[pl.ds(0, NG - 1)], phase)

        @pl.when(jnp.logical_not(is_diag))
        def _():
            got(dst, phase)

    def sent_columns(dst, phase):
        @pl.when(is_diag)
        def _():
            sent(dst.at[pl.ds(0, NG - 1)], phase)

        @pl.when(jnp.logical_not(is_diag))
        def _():
            sent(dst, phase)

    def scatter_z(src, dst, phase):
        for i in range(1, NZ):
            to = (z + i) % NZ
            send(src.at[to], dst.at[z], phase, to * NG + g, m)
        dst[z] = src[z]

    def gather_z(fin, phase):
        for i in range(1, NZ):
            to = (z + i) % NZ
            send(fin.at[g, z], fin.at[g, z], phase, to * NG + g, m)

    def y_copy(fin, at, to, k):
        return pltpu.make_async_remote_copy(
            src_ref=fin.at[at], dst_ref=fin.at[at], send_sem=y_s.at[k], recv_sem=y_r.at[k],
            device_id=(z * NG + to * 2 + c, m), device_id_type=MESH,
        )

    def c_copy(fin, at, k):
        return pltpu.make_async_remote_copy(
            src_ref=fin.at[at], dst_ref=fin.at[at], send_sem=c_s.at[k], recv_sem=c_r.at[k],
            device_id=(z * NG + y * 2 + 1 - c, m), device_id_type=MESH,
        )

    bar = pltpu.get_barrier_semaphore()
    over(DP, lambda i: pl.semaphore_signal(bar, inc=1, device_id=((d + i) % DP, m), device_id_type=MESH))
    for i in range(1, MP):
        pl.semaphore_signal(bar, inc=1, device_id=(d, (m + i) % MP), device_id_type=MESH)

    def greet(i, carry):
        @pl.when(jnp.logical_not(jnp.logical_and(is_diag, i == g)))
        def _():
            pl.semaphore_signal(bar, inc=1, device_id=(z * NG + i, g // 2), device_id_type=MESH)

        return carry

    lax.fori_loop(0, NG, greet, 0)

    first = dot(pooled[...], w_out[...])
    for j in range(MP):
        part[j] = first[:NODE, j * COLS : (j + 1) * COLS]
    e2[...] = jnp.zeros_like(e2)
    m2[...] = jnp.zeros_like(m2)
    pool_g[g] = pooled[...]

    pl.semaphore_wait(bar, DP - 1 + MP - 1 + 2 * MP - is_diag.astype(jnp.int32))

    to_mp(part, sums, POOL_SUM)
    to_dp(want, asked, ASK)
    got(sums.at[pl.ds(0, MP - 1)], POOL_SUM)
    embed = tmean[...] + (sums[0] + sums[1] + sums[2] + sums[3])
    embed = pad_rows(embed, PAD).astype(BF16)
    e2[0:PAD, :] = embed[:, :128]
    e2[PAD : 2 * PAD, :] = embed[:, 128:]
    emb_g[g] = embed

    got(asked.at[pl.ds(0, DP - 1)], ASK)
    names = asked[...].reshape(DP * SLOT, 128).astype(F32)
    sel = (names == iota((DP * SLOT, 128), 1).astype(F32)).astype(F32)
    sbuf[...] = dot(sel.astype(BF16), e2[...]).astype(BF16).reshape(DP, SLOT, 128)
    to_dp(sbuf, rbuf, ROWS)
    to_group(emb_g, EMB_G)
    to_group(pool_g, POOL_G)
    sel_t[...] = jnp.transpose(sel)[: 2 * PAD].astype(BF16)
    zself = dot(embed, w_self[...])
    got(rbuf.at[pl.ds(0, DP - 1)], ROWS)
    two = dot(gh[...], rbuf[...].reshape(DP * SLOT, 128))
    agg = (jnp.concatenate([two[:PAD], two[PAD:]], axis=1) / cnt[...]).astype(BF16)
    zfull = zself + dot(agg, w_neigh[...])
    for j in range(MP):
        zpart[j] = zfull[:NODE, j * COLS : (j + 1) * COLS]
    to_mp(zpart, zsums, Z_SUM)
    agg_g[g] = agg
    to_group(agg_g, AGG_G)
    got(zsums.at[pl.ds(0, MP - 1)], Z_SUM)
    zc = zsums[0] + zsums[1] + zsums[2] + zsums[3]

    root = math.sqrt(2.0 / math.pi)
    th = jnp.tanh(root * (zc + 0.044715 * (zc * zc * zc)))
    cdf = 0.5 * (1.0 + th)
    slope = cdf + zc * (0.5 * (1.0 - th * th) * (root * (1.0 + (3 * 0.044715) * (zc * zc))))
    dz = pad_rows(cot[...].astype(F32) * slope, PAD).astype(BF16)
    dzf[m] = dz
    for i in range(1, MP):
        send(dzf.at[m], dzf.at[m], DZ, d, (m + i) % MP)
    dz2[0] = dz[:, :128]
    dz2[1] = dz[:, 128:]
    to_columns(dz2, dz_g, DZ_G)
    mixed[...] = (zc * cdf).astype(BF16)
    got(dzf.at[pl.ds(0, MP - 1)], DZ)

    dagg = dot_nt(dzf[0], w_neigh[:, 0:COLS])
    for j in range(1, MP):
        dagg = dagg + dot_nt(dzf[j], w_neigh[:, j * COLS : (j + 1) * COLS])
    msg = (dagg / cnt[...]).astype(BF16)
    m2[0:PAD, :] = msg[:, :128]
    m2[PAD : 2 * PAD, :] = msg[:, 128:]
    sbuf2[...] = dot(ght[...], m2[...]).astype(BF16).reshape(DP, SLOT, 128)
    to_dp(sbuf2, rbuf2, BACK)
    own = dot_nt(dzf[0], w_self[:, 0:COLS])
    for j in range(1, MP):
        own = own + dot_nt(dzf[j], w_self[:, j * COLS : (j + 1) * COLS])

    got_columns(dz_g, DZ_G)
    got(emb_g.at[pl.ds(0, NG - 1)], EMB_G)
    got(agg_g.at[pl.ds(0, NG - 1)], AGG_G)
    rhs = dz_g[...].reshape(NG * PAD, 128)
    sn_s[:, 0] = dot_tn(emb_g[...].reshape(NG * PAD, COLS), rhs).astype(BF16).reshape(NZ, PAD, 128)
    sn_s[:, 1] = dot_tn(agg_g[...].reshape(NG * PAD, COLS), rhs).astype(BF16).reshape(NZ, PAD, 128)
    scatter_z(sn_s, sn_r, SN_RS)

    got(rbuf2.at[pl.ds(0, DP - 1)], BACK)
    two = dot(sel_t[...], rbuf2[...].reshape(DP * SLOT, 128))
    grad = (own + jnp.concatenate([two[:PAD], two[PAD:]], axis=1)).astype(BF16)
    ng2[0] = grad[:, :128]
    ng2[1] = grad[:, 128:]
    to_columns(ng2, ng_g, NG_G)
    ngrad[...] = grad[:NODE]

    factor = 1.0 / math.sqrt(NODE * DP)

    def z_total(buf):
        total = buf[0].astype(F32)
        for i in range(1, NZ):
            total = total + buf[i].astype(F32)
        return (total * factor).astype(BF16)

    got(sn_r.at[pl.ds(0, NZ - 1)], SN_RS)
    fin_sn[g, z] = z_total(sn_r)
    gather_z(fin_sn, SN_AG)

    got(pool_g.at[pl.ds(0, NG - 1)], POOL_G)
    got_columns(ng_g, NG_G)
    out = dot_tn(pool_g[...].reshape(NG * PAD, COLS), ng_g[...].reshape(NG * PAD, 128))
    out_s[...] = out.astype(BF16).reshape(NZ, PAD, 128)
    scatter_z(out_s, out_r, OUT_RS)

    got(fin_sn.at[0, pl.ds(0, NZ - 1)], SN_AG)
    for i in range(1, NY):
        y_copy(fin_sn, g, (y + i) % NY, i - 1).start()
    c_copy(fin_sn, g, 0).start()

    got(out_r.at[pl.ds(0, NZ - 1)], OUT_RS)
    fin_out[g, z] = z_total(out_r)
    gather_z(fin_out, OUT_AG)

    def forward(fin, first):
        for i in range(1, NY):
            at = ((y + NY - i) % NY) * 2 + c
            y_copy(fin, at, y, first + i - 1).wait_recv()
            c_copy(fin, at, (first // 3) * 4 + i).start()

    forward(fin_sn, 0)
    got(fin_out.at[0, pl.ds(0, NZ - 1)], OUT_AG)
    for i in range(1, NY):
        y_copy(fin_out, g, (y + i) % NY, 3 + i - 1).start()
    c_copy(fin_out, g, 4).start()

    for i in range(NY):
        c_copy(fin_sn, ((y + NY - i) % NY) * 2 + 1 - c, i).wait_recv()
    for j in range(NG):
        cols = slice(j * 128, j * 128 + 128)
        o_self[:, cols] = fin_sn[j, :, 0].reshape(COLS, 128).astype(F32)
        o_neigh[:, cols] = fin_sn[j, :, 1].reshape(COLS, 128).astype(F32)

    forward(fin_out, 3)
    for i in range(NY):
        c_copy(fin_out, ((y + NY - i) % NY) * 2 + 1 - c, 4 + i).wait_recv()
    for j in range(NG):
        o_out[:, j * 128 : j * 128 + 128] = fin_out[j].reshape(COLS, 128).astype(F32)

    sent(sums.at[pl.ds(0, MP - 1)], POOL_SUM)
    sent(asked.at[pl.ds(0, DP - 1)], ASK)
    sent(rbuf.at[pl.ds(0, DP - 1)], ROWS)
    sent(emb_g.at[pl.ds(0, NG - 1)], EMB_G)
    sent(pool_g.at[pl.ds(0, NG - 1)], POOL_G)
    sent(agg_g.at[pl.ds(0, NG - 1)], AGG_G)
    sent(zsums.at[pl.ds(0, MP - 1)], Z_SUM)
    sent(dzf.at[pl.ds(0, MP - 1)], DZ)
    sent_columns(dz_g, DZ_G)
    sent(rbuf2.at[pl.ds(0, DP - 1)], BACK)
    sent_columns(ng_g, NG_G)
    sent(sn_r.at[pl.ds(0, NZ - 1)], SN_RS)
    sent(fin_sn.at[0, pl.ds(0, NZ - 1)], SN_AG)
    sent(out_r.at[pl.ds(0, NZ - 1)], OUT_RS)
    sent(fin_out.at[0, pl.ds(0, NZ - 1)], OUT_AG)
    for k in range(3):
        y_copy(fin_sn, g, y, k).wait_send()
        y_copy(fin_out, g, y, 3 + k).wait_send()
    for k in range(NY):
        c_copy(fin_sn, g, k).wait_send()
        c_copy(fin_out, g, 4 + k).wait_send()


def graph(pooled, tmean, want, gh, ght, cnt, w_out, w_self, w_neigh, cot):
    vmem = pl.BlockSpec(memory_space=pltpu.VMEM)
    return pl.pallas_call(
        graph_kernel,
        out_shape=[
            jax.ShapeDtypeStruct((NODE, COLS), BF16),
            jax.ShapeDtypeStruct((NODE, COLS), BF16),
            jax.ShapeDtypeStruct((COLS, WIDTH), F32),
            jax.ShapeDtypeStruct((COLS, WIDTH), F32),
            jax.ShapeDtypeStruct((COLS, WIDTH), F32),
        ],
        in_specs=[vmem] * 10,
        out_specs=[vmem] * 5,
        scratch_shapes=[
            pltpu.VMEM((DP, SLOT, 128), BF16),
            pltpu.VMEM((DP, SLOT, 128), BF16),
            pltpu.VMEM((DP, SLOT, 128), BF16),
            pltpu.VMEM((DP, SLOT, 128), BF16),
            pltpu.VMEM((DP, SLOT, 128), BF16),
            pltpu.VMEM((2 * PAD, DP * SLOT), BF16),
            pltpu.VMEM((MP, NODE, COLS), F32),
            pltpu.VMEM((MP, NODE, COLS), F32),
            pltpu.VMEM((MP, NODE, COLS), F32),
            pltpu.VMEM((MP, NODE, COLS), F32),
            pltpu.VMEM((128, 128), BF16),
            pltpu.VMEM((128, 128), BF16),
            pltpu.VMEM((NG, PAD, COLS), BF16),
            pltpu.VMEM((NG, PAD, COLS), BF16),
            pltpu.VMEM((NG, PAD, COLS), BF16),
            pltpu.VMEM((MP, PAD, COLS), BF16),
            pltpu.VMEM((2, PAD, 128), BF16),
            pltpu.VMEM((NG, PAD, 128), BF16),
            pltpu.VMEM((2, PAD, 128), BF16),
            pltpu.VMEM((NG, PAD, 128), BF16),
            pltpu.VMEM((NZ, 2, PAD, 128), BF16),
            pltpu.VMEM((NZ, 2, PAD, 128), BF16),
            pltpu.VMEM((NG, NZ, 2, PAD, 128), BF16),
            pltpu.VMEM((NZ, PAD, 128), BF16),
            pltpu.VMEM((NZ, PAD, 128), BF16),
            pltpu.VMEM((NG, NZ, PAD, 128), BF16),
            pltpu.SemaphoreType.DMA((15,)),
            pltpu.SemaphoreType.DMA((15,)),
            pltpu.SemaphoreType.DMA((6,)),
            pltpu.SemaphoreType.DMA((6,)),
            pltpu.SemaphoreType.DMA((8,)),
            pltpu.SemaphoreType.DMA((8,)),
        ],
        compiler_params=pltpu.CompilerParams(
            collective_id=0, has_side_effects=True, vmem_limit_bytes=40 * 2**20
        ),
        cost_estimate=pl.CostEstimate(flops=10**9, bytes_accessed=8 * 10**6, transcendentals=10**4),
    )(pooled, tmean, want.reshape(DP, SLOT, 128), gh, ght, cnt, w_out, w_self, w_neigh, cot)


def per_device(texts, w_qkv, w_out, w_self, w_neigh, neighbours, cotangent):
    pooled, tmean, want, gh, ght, cnt = attention(texts, w_qkv, neighbours)
    return tuple(graph(pooled, tmean, want, gh, ght, cnt, w_out, w_self, w_neigh, cotangent))


def solution(mesh):
    return jax.shard_map(
        per_device,
        mesh=mesh,
        in_specs=(
            P("dp", None, None),
            P(None, "mp"),
            P("mp", None),
            P("mp", None),
            P("mp", None),
            P("dp", None),
            P("dp", "mp"),
        ),
        out_specs=(P("dp", "mp"), P("dp", "mp"), P("mp", None), P("mp", None), P("mp", None)),
        check_vma=False,
    )
```

time: 387 us -> 104 us (0.27)
  waiting for transfers between devices: 250 us -> 0 us
  Pallas kernels: 0 us -> 94.4 us
  starting transfers between devices: 41.8 us -> 0 us
  matrix products: 24.7 us -> 0 us
  other arithmetic: 21.1 us -> 0 us
  blocking collectives: 18 us -> 0 us
  between operations: 14 us -> 0.69 us
  local copies, waits for them, and re-layouts: 15.4 us -> 9.09 us
    psum x2 -> x0, waiting for transfers between devices: 206 us -> none  [the longest x1 188 us: per_device(): lax.psum((local_self, local_neigh, local_out), 'dp')]
    pallas_call x0 -> x2, Pallas kernels: none -> 94.4 us  [the longest x1 73.7 us: graph(): pl.pallas_call(graph_kernel, out_shape=[jax.ShapeDtypeStruct((NODE, COLS)...]
    all_to_all x3 -> x0, starting transfers between devices: 41.7 us -> none  [the longest x1 15.8 us: per_device(): lax.all_to_all(slot_msgs.reshape(groups, limit, cols), 'dp', split_axis=0...]
    all_to_all x3 -> x0, waiting for transfers between devices: 29.1 us -> none  [the longest x1 12.7 us: per_device(): lax.all_to_all(sending.reshape(groups, limit, cols), 'dp', split_axis=0,...]
    dot_general x14 -> x0, matrix products: 24.7 us -> none  [the longest x1 9.46 us: per_device(): jnp.einsum('nld,de->nle', texts, w_qkv, preferred_element_type=jnp.float32)]
    all_gather x2 -> x0, blocking collectives: 18 us -> none  [the longest x1 9.03 us: per_device(): grad_full = lax.all_gather(node_grad, 'mp', axis=1, tiled=True)]
    reduce_scatter x1 -> x0, waiting for transfers between devices: 15.3 us -> none  [per_device(): z_cols = lax.psum_scatter(partial_z, 'mp', scatter_dimension=1, tiled=True)]
    unnamed x15 -> x18, local copies, waits for them, and re-layouts: 1.49 us -> 9.09 us
  transfers between devices with their start and end apart: 6 -> 0, of which waited for: 6 -> 0; matrix products, arithmetic and copies ran while one was open for 3% -> 0% of each run, Pallas kernels for 0% -> 0%
where the time goes in v1:
time: 104 us
  Pallas kernels  94.4 us (91%)
  local copies, waits for them, and re-layouts  9.09 us (9%)
    pallas_call x1, Pallas kernels, graph(): pl.pallas_call(graph_kernel, out_shape=[jax.ShapeDtypeStruct((NODE, COLS)...  73.7 us
    pallas_call x1, Pallas kernels, attention(): pl.pallas_call(attention_kernel, grid=(steps,), out_shape=[jax.ShapeDtype...  20.7 us
    unnamed x18, local copies, waits for them, and re-layouts  9.09 us

profile of v1, /device:TPU:1, one launch (start us, length us, event | category | flops | bytes accessed | tf_op | source)
XLA Modules:
  0.0 104.2 jit_solution(8372496522925751784)
XLA Ops:
  0.6 0.8 copy.12.nb_ref
  1.4 0.0 copy-start
  1.4 2.8 %copy-done = bf16[24,128,1024]{2,1,0:T(8,128)(2,1)S(1)} copy-done((bf16[24,128,1024]{2,1,0:T(8,128)(2,1)S(1)}, bf16[24,128,1024]{2,1,0:T(8,128)(2,1)}, u32[]{:S(2)}) %copy-start) | copy-done | bytes 6291480
  4.2 0.0 copy-start.1
  4.2 1.4 %copy-done.1 = bf16[1024,768]{1,0:T(8,128)(2,1)S(1)} copy-done((bf16[1024,768]{1,0:T(8,128)(2,1)S(1)}, bf16[1024,768]{1,0:T(8,128)(2,1)}, u32[]{:S(2)}) %copy-start.1) | copy-done | bytes 1572888
  5.6 0.0 copy-start.2
  5.6 0.0 copy-start.3
  5.6 0.0 copy-start.4
  5.6 0.0 copy-start.5
  5.6 20.7 %shard_map.110 = (bf16[32,256]{1,0:T(8,128)(2,1)S(1)}, f32[24,256]{1,0:T(8,128)S(1)}, bf16[1024,128]{1,0:T(8,128)(2,1)S(1)}, bf16[64,1024]{1,0:T(8,128)(2,1)S(1)...) custom-call(bf16[24,128,1024]{2,1,0:T(8,128)(2,1)S(1)} %copy-done, bf16[1024,768]{1,0:T(8,128)(2,1)S(1)} %copy-done.1, ...), custom_call_target="tpu_custom_call" | custom-call | flops 6000000000 | bytes 9000000 | tf_op jit(solution)/shard_map/pallas_call | solution.py:133
  26.3 0.0 copy-done.2
  26.3 0.0 copy-done.3
  26.3 0.0 copy-done.4
  26.4 0.0 copy-done.5
  26.4 73.7 %shard_map.111 = (bf16[24,256]{1,0:T(8,128)(2,1)S(1)}, bf16[24,256]{1,0:T(8,128)(2,1)S(1)}, f32[256,1024]{1,0:T(8,128)S(1)}, f32[256,1024]{1,0:T(8,128)S(1)}, f32[256,1024]{1,0:T(8,128)S(1)}) custom-call(bf16[32,256]{1,0:T(8,128)(2,1)S(1)} %get-tuple-element.11.pooled, f32[24,256]{1,0:T(8,128)S(1)} %get-tuple-element.12.tmean, ...), custom_call_target="tpu_custom_call" | custom-call | flops 1000000000 | bytes 8000000 | tf_op jit(solution)/shard_map/pallas_call | solution.py:452
  100.1 0.6 copy.18
  100.7 0.6 copy.19
  101.3 1.0 copy.20
  102.3 1.0 copy.21
  103.2 1.0 copy.22
Async XLA Ops:
  1.4 2.8 %copy-start = (bf16[24,128,1024]{2,1,0:T(8,128)(2,1)S(1)}, bf16[24,128,1024]{2,1,0:T(8,128)(2,1)}, u32[]{:S(2)}) copy-start(bf16[24,128,1024]{2,1,0:T(8,128)(2,1)} %tx_ref.1) | copy-start | bytes 18874372
  4.2 1.4 %copy-start.1 = (bf16[1024,768]{1,0:T(8,128)(2,1)S(1)}, bf16[1024,768]{1,0:T(8,128)(2,1)}, u32[]{:S(2)}) copy-start(bf16[1024,768]{1,0:T(8,128)(2,1)} %w_ref.1) | copy-start | bytes 4718596
  5.6 20.7 %copy-start.2 = (bf16[256,1024]{1,0:T(8,128)(2,1)S(1)}, bf16[256,1024]{1,0:T(8,128)(2,1)}, u32[]{:S(2)}) copy-start(bf16[256,1024]{1,0:T(8,128)(2,1)} %w_out.1) | copy-start | bytes 1572868
  5.6 20.7 %copy-start.3 = (bf16[256,1024]{1,0:T(8,128)(2,1)S(1)}, bf16[256,1024]{1,0:T(8,128)(2,1)}, u32[]{:S(2)}) copy-start(bf16[256,1024]{1,0:T(8,128)(2,1)} %w_self.1) | copy-start | bytes 1572868
  5.6 20.7 %copy-start.4 = (bf16[256,1024]{1,0:T(8,128)(2,1)S(1)}, bf16[256,1024]{1,0:T(8,128)(2,1)}, u32[]{:S(2)}) copy-start(bf16[256,1024]{1,0:T(8,128)(2,1)} %w_neigh.1) | copy-start | bytes 1572868
  5.6 20.8 %copy-start.5 = (bf16[24,256]{1,0:T(8,128)(2,1)S(1)}, bf16[24,256]{1,0:T(8,128)(2,1)}, u32[]{:S(2)}) copy-start(bf16[24,256]{1,0:T(8,128)(2,1)} %cot.1) | copy-start | bytes 36868

commit v2 on v1

v2 whole, which is shorter than its diff:
```python
import math

import jax
import jax.numpy as jnp
from jax import lax
from jax.experimental import pallas as pl
from jax.experimental.pallas import tpu as pltpu
from jax.sharding import PartitionSpec as P

MESH = pl.DeviceIdType.MESH
F32, BF16 = jnp.float32, jnp.bfloat16
HD = 64
NODE = 24
PAD = 32
DP, MP, NZ, NG, NY = 64, 4, 8, 8, 4
COLS, WIDTH = 256, 1024
SLOT = 16
EMPTY = 120.0
VMEM_LIMIT = 60 * 2**20
TEXTS = 8


def dot(a, b):
    return jnp.dot(a, b, preferred_element_type=F32)


def dot_nt(a, b):
    return lax.dot_general(a, b, (((1,), (1,)), ((), ())), preferred_element_type=F32)


def dot_tn(a, b):
    return lax.dot_general(a, b, (((0,), (0,)), ((), ())), preferred_element_type=F32)


def iota(shape, dim):
    return lax.broadcasted_iota(jnp.int32, shape, dim)


def pad_rows(x, rows):
    return jnp.concatenate([x, jnp.zeros((rows - x.shape[0], x.shape[1]), x.dtype)], axis=0)


def routing(ids_ref, want, gh, ght, cnt_out):
    ids = jnp.transpose(ids_ref[...].astype(F32))
    own = jnp.floor((ids + 0.5) * (1.0 / NODE))
    loc = ids - NODE * own
    live = ids >= 0.0
    cnt = jnp.maximum(jnp.sum(live.astype(F32), axis=1, keepdims=True), 1.0)
    cnt_out[...] = jnp.concatenate(
        [jnp.broadcast_to(cnt, (NODE, COLS)), jnp.ones((PAD - NODE, COLS), F32)], axis=0
    )
    fan = ids.shape[1]
    groups = iota((NODE, DP), 1).astype(F32)
    hots = [(own[:, f : f + 1] == groups).astype(F32) for f in range(fan)]
    total = hots[0]
    for f in range(1, fan):
        total = total + hots[f]
    lower = (iota((NODE, NODE), 1) < iota((NODE, NODE), 0)).astype(BF16)
    run = dot(lower, total.astype(BF16))
    spots = iota((NODE, DP * SLOT), 1).astype(F32)
    left = jnp.zeros((NODE, DP * SLOT), F32)
    right = jnp.zeros((NODE, DP * SLOT), F32)
    names = jnp.zeros((NODE, DP * SLOT), F32)
    for f in range(fan):
        rank = jnp.sum(hots[f] * run, axis=1, keepdims=True)
        run = run + hots[f]
        at = jnp.where(live[:, f : f + 1], own[:, f : f + 1] * SLOT + rank, -1000.0)
        name = loc[:, f : f + 1]
        is_left = spots == at
        is_right = spots == at + 8.0
        left = left + is_left.astype(F32)
        right = right + is_right.astype(F32)
        names = names + jnp.where(is_left, name - EMPTY, 0.0)
        names = names + jnp.where(is_right, name + (PAD - EMPTY), 0.0)
    gap = jnp.zeros((PAD - NODE, DP * SLOT), F32)
    both = jnp.concatenate([left, gap, right, gap], axis=0)
    gh[...] = both.astype(BF16)
    ght[...] = jnp.transpose(pad_rows(both, 128)).astype(BF16)
    spread = jnp.transpose(pad_rows(names, 128)).astype(BF16)
    want[...] = (dot(spread, jnp.ones((128, 128), BF16)) + EMPTY).astype(BF16).reshape(DP, SLOT, 128)


def order_columns(w, wp):
    low = iota((1, 128), 1) < HD
    for pair in range(2):
        base = pair * 384
        at = pair * 128
        a = w[:, base : base + 128].astype(F32)
        b = w[:, base + 128 : base + 256].astype(F32)
        c = w[:, base + 256 : base + 384].astype(F32)
        wp[:, at : at + 128] = jnp.where(low, a, b).astype(BF16)
        wp[:, 256 + at : 384 + at] = pltpu.roll(jnp.where(low, c, a), HD, 1).astype(BF16)
        wp[:, 512 + at : 640 + at] = jnp.where(low, b, c).astype(BF16)


def attend(qkv):
    low = iota((1, 128), 1) < HD
    scale = 1.0 / (math.sqrt(HD) * math.log(2.0))
    zero = jnp.zeros((), BF16)
    texts = []
    for t in range(TEXTS):
        rows = slice(t * 128, t * 128 + 128)
        parts = []
        for pair in range(2):
            at = pair * 128
            qt = qkv[rows, at : at + 128]
            kt = qkv[rows, 256 + at : 384 + at]
            vt = qkv[rows, 512 + at : 640 + at].astype(F32)
            two = jnp.concatenate([jnp.where(low, qt, zero), jnp.where(low, zero, qt)], axis=0)
            s = dot_nt(kt, two)
            e = jnp.exp2((s - jnp.max(s, axis=0, keepdims=True)) * scale)
            p = (e * (1.0 / jnp.sum(e, axis=0, keepdims=True))).astype(BF16).astype(F32)
            first = jnp.sum(p[:, :128], axis=1, keepdims=True)
            second = jnp.sum(p[:, 128:], axis=1, keepdims=True)
            parts.append(jnp.sum(jnp.where(low, first, second) * vt, axis=0, keepdims=True))
        texts.append(jnp.concatenate(parts, axis=1))
    return jnp.concatenate(texts, axis=0) * (1.0 / 128)


ASK, POOL_SUM, ROWS, EMB_G, POOL_G, AGG_G, Z_SUM, DZ, DZ_G, BACK, NG_G, SN_RS, SN_AG, OUT_RS, OUT_AG = range(15)


def step_kernel(
    texts_in, qkv_in, out_in, self_in, neigh_in, ids_in, cot_in,
    o_mixed, o_ngrad, o_sn, o_out,
    mixed, ngrad, fin_sn, fin_out, tx, wq, wp, qkv, w_out, w_self, w_neigh, ids, cot, acc, tmean, pooled, want, gh, ght, cnt,
    asked, sbuf, rbuf, sbuf2, rbuf2, sel_t, part, sums, zpart, zsums, e2, m2,
    emb_g, pool_g, agg_g, dzf, dz2, dz_g, ng2, ng_g, sn_s, sn_r, out_s, out_r,
    tsem, lsem, osem, ssem, rsem, y_s, y_r, c_s, c_r,
):
    m, d = lax.axis_index("mp"), lax.axis_index("dp")
    z, g = d // NG, d % NG
    y, c = g // 2, g % 2
    is_diag = (g // 2) == m

    def send(src, dst, phase, dp, mp):
        pltpu.make_async_remote_copy(
            src_ref=src, dst_ref=dst, send_sem=ssem.at[phase], recv_sem=rsem.at[phase],
            device_id=(dp, mp), device_id_type=MESH,
        ).start()

    def got(ref, phase):
        pltpu.make_async_copy(ref, ref, rsem.at[phase]).wait()

    def sent(ref, phase):
        pltpu.make_async_copy(ref, ref, ssem.at[phase]).wait()

    pending = []

    def emit(k, src, dst):
        copy = pltpu.make_async_copy(src, dst, osem.at[k])
        copy.start()
        pending.append(copy.wait)

    def later(ref, phase):
        pending.append(lambda: sent(ref, phase))

    def over(count, body):
        def step(i, carry):
            body(i)
            return carry

        lax.fori_loop(1, count, step, 0)

    def to_dp(src, dst, phase):
        for k in (4, 3, 5, 2, 6, 1, 7, 0):

            def one(i, carry):
                to = ((z + k) % NZ) * NG + (g + i) % NG
                send(src.at[to], dst.at[d], phase, to, m)
                return carry

            lax.fori_loop(1 if k == 0 else 0, NG, one, 0)
        dst[d] = src[d]
        later(dst.at[pl.ds(0, DP - 1)], phase)

    def to_mp(src, dst, phase):
        for i in range(1, MP):
            to = (m + i) % MP
            send(src.at[to], dst.at[m], phase, d, to)
        dst[m] = src[m]
        later(dst.at[pl.ds(0, MP - 1)], phase)

    def to_group(block, phase):
        for i in range(1, NG):
            send(block.at[g], block.at[g], phase, z * NG + (g + i) % NG, m)
        later(block.at[pl.ds(0, NG - 1)], phase)

    def to_columns(src, dst, phase):
        def one(i, carry):
            mp, half = i // 2, i % 2
            at = 2 * m + half
            here = jnp.logical_and(mp == m, at == g)

            @pl.when(jnp.logical_not(here))
            def _():
                send(src.at[half], dst.at[g], phase, z * NG + at, mp)

            @pl.when(here)
            def _():
                dst[g] = src[half]

            return carry

        lax.fori_loop(0, 2 * MP, one, 0)
        pending.append(lambda: sent_columns(dst, phase))

    def got_columns(dst, phase):
        @pl.when(is_diag)
        def _():
            got(dst.at[pl.ds(0, NG - 1)], phase)

        @pl.when(jnp.logical_not(is_diag))
        def _():
            got(dst, phase)

    def sent_columns(dst, phase):
        @pl.when(is_diag)
        def _():
            sent(dst.at[pl.ds(0, NG - 1)], phase)

        @pl.when(jnp.logical_not(is_diag))
        def _():
            sent(dst, phase)

    def scatter_z(src, dst, phase):
        for i in range(1, NZ):
            to = (z + i) % NZ
            send(src.at[to], dst.at[z], phase, to * NG + g, m)
        dst[z] = src[z]
        later(dst.at[pl.ds(0, NZ - 1)], phase)

    def gather_z(fin, phase):
        for i in range(1, NZ):
            to = (z + i) % NZ
            send(fin.at[g, z], fin.at[g, z], phase, to * NG + g, m)
        later(fin.at[0, pl.ds(0, NZ - 1)], phase)

    def y_copy(fin, at, to, k):
        return pltpu.make_async_remote_copy(
            src_ref=fin.at[at], dst_ref=fin.at[at], send_sem=y_s.at[k], recv_sem=y_r.at[k],
            device_id=(z * NG + to * 2 + c, m), device_id_type=MESH,
        )

    def c_copy(fin, at, k):
        return pltpu.make_async_remote_copy(
            src_ref=fin.at[at], dst_ref=fin.at[at], send_sem=c_s.at[k], recv_sem=c_r.at[k],
            device_id=(z * NG + y * 2 + 1 - c, m), device_id_type=MESH,
        )

    def y_sends(fin, first):
        for i in range(1, NY):
            copy = y_copy(fin, g, (y + i) % NY, first + i - 1)
            copy.start()
            pending.append(copy.wait_send)
        own = c_copy(fin, g, (first // 3) * 4)
        own.start()
        pending.append(own.wait_send)

    weight = pltpu.make_async_copy(qkv_in, wq, lsem.at[0])
    names_in = pltpu.make_async_copy(ids_in, ids, lsem.at[1])
    names_in.start()
    weight.start()
    chunks = NODE // TEXTS

    def chunk(i):
        rows = pl.ds(i * TEXTS, TEXTS)
        return pltpu.make_async_copy(texts_in.at[rows], tx.at[rows], tsem.at[i])

    for i in range(chunks):
        chunk(i).start()
    others = [
        pltpu.make_async_copy(src, dst, lsem.at[2 + i])
        for i, (src, dst) in enumerate(
            [(out_in, w_out), (self_in, w_self), (neigh_in, w_neigh), (cot_in, cot)]
        )
    ]
    for copy in others:
        copy.start()

    bar = pltpu.get_barrier_semaphore()
    over(DP, lambda i: pl.semaphore_signal(bar, inc=1, device_id=((d + i) % DP, m), device_id_type=MESH))
    for i in range(1, MP):
        pl.semaphore_signal(bar, inc=1, device_id=(d, (m + i) % MP), device_id_type=MESH)

    def greet(i, carry):
        @pl.when(jnp.logical_not(jnp.logical_and(is_diag, i == g)))
        def _():
            pl.semaphore_signal(bar, inc=1, device_id=(z * NG + i, g // 2), device_id_type=MESH)

        return carry

    lax.fori_loop(0, NG, greet, 0)

    names_in.wait()
    routing(ids, want, gh, ght, cnt)
    e2[...] = jnp.zeros_like(e2)
    m2[...] = jnp.zeros_like(m2)
    weight.wait()
    order_columns(wq, wp)
    pl.semaphore_wait(bar, DP - 1 + MP - 1 + 2 * MP - is_diag.astype(jnp.int32))
    to_dp(want, asked, ASK)

    def work(i, carry):
        chunk(i).wait()
        rows = pl.ds(pl.multiple_of(i * TEXTS, TEXTS), TEXTS)
        qkv[...] = dot(tx[rows].reshape(TEXTS * 128, WIDTH), wp[...]).astype(BF16)
        acc[rows, :] = attend(qkv)
        mine = tx[rows, :, pl.ds(pl.multiple_of(m * COLS, COLS), COLS)]
        tmean[rows, :] = jnp.sum(mine.astype(F32), axis=1) * (1.0 / 128)
        return carry

    lax.fori_loop(0, chunks, work, 0)
    for copy in others:
        copy.wait()
    pooled[...] = pad_rows(acc[...], PAD).astype(BF16)
    pool_g[g] = pooled[...]
    first = dot(pooled[...], w_out[...])
    for j in range(MP):
        part[j] = first[:NODE, j * COLS : (j + 1) * COLS]

    to_mp(part, sums, POOL_SUM)
    got(sums.at[pl.ds(0, MP - 1)], POOL_SUM)
    embed = tmean[...] + (sums[0] + sums[1] + sums[2] + sums[3])
    embed = pad_rows(embed, PAD).astype(BF16)
    e2[0:PAD, :] = embed[:, :128]
    e2[PAD : 2 * PAD, :] = embed[:, 128:]
    emb_g[g] = embed

    got(asked.at[pl.ds(0, DP - 1)], ASK)
    names = asked[...].reshape(DP * SLOT, 128).astype(F32)
    sel = (names == iota((DP * SLOT, 128), 1).astype(F32)).astype(F32)
    sbuf[...] = dot(sel.astype(BF16), e2[...]).astype(BF16).reshape(DP, SLOT, 128)
    to_dp(sbuf, rbuf, ROWS)
    to_group(emb_g, EMB_G)
    to_group(pool_g, POOL_G)
    sel_t[...] = jnp.transpose(sel)[: 2 * PAD].astype(BF16)
    zself = dot(embed, w_self[...])
    got(rbuf.at[pl.ds(0, DP - 1)], ROWS)
    two = dot(gh[...], rbuf[...].reshape(DP * SLOT, 128))
    agg = (jnp.concatenate([two[:PAD], two[PAD:]], axis=1) / cnt[...]).astype(BF16)
    zfull = zself + dot(agg, w_neigh[...])
    for j in range(MP):
        zpart[j] = zfull[:NODE, j * COLS : (j + 1) * COLS]
    to_mp(zpart, zsums, Z_SUM)
    agg_g[g] = agg
    to_group(agg_g, AGG_G)
    got(zsums.at[pl.ds(0, MP - 1)], Z_SUM)
    zc = zsums[0] + zsums[1] + zsums[2] + zsums[3]

    root = math.sqrt(2.0 / math.pi)
    th = jnp.tanh(root * (zc + 0.044715 * (zc * zc * zc)))
    cdf = 0.5 * (1.0 + th)
    slope = cdf + zc * (0.5 * (1.0 - th * th) * (root * (1.0 + (3 * 0.044715) * (zc * zc))))
    dz = pad_rows(cot[...].astype(F32) * slope, PAD).astype(BF16)
    dzf[m] = dz
    for i in range(1, MP):
        send(dzf.at[m], dzf.at[m], DZ, d, (m + i) % MP)
    later(dzf.at[pl.ds(0, MP - 1)], DZ)
    dz2[0] = dz[:, :128]
    dz2[1] = dz[:, 128:]
    to_columns(dz2, dz_g, DZ_G)
    mixed[...] = (zc * cdf).astype(BF16)
    emit(0, mixed, o_mixed)
    got(dzf.at[pl.ds(0, MP - 1)], DZ)

    dagg = dot_nt(dzf[0], w_neigh[:, 0:COLS])
    for j in range(1, MP):
        dagg = dagg + dot_nt(dzf[j], w_neigh[:, j * COLS : (j + 1) * COLS])
    msg = (dagg / cnt[...]).astype(BF16)
    m2[0:PAD, :] = msg[:, :128]
    m2[PAD : 2 * PAD, :] = msg[:, 128:]
    sbuf2[...] = dot(ght[...], m2[...]).astype(BF16).reshape(DP, SLOT, 128)
    to_dp(sbuf2, rbuf2, BACK)
    own = dot_nt(dzf[0], w_self[:, 0:COLS])
    for j in range(1, MP):
        own = own + dot_nt(dzf[j], w_self[:, j * COLS : (j + 1) * COLS])

    got_columns(dz_g, DZ_G)
    got(emb_g.at[pl.ds(0, NG - 1)], EMB_G)
    got(agg_g.at[pl.ds(0, NG - 1)], AGG_G)
    rhs = dz_g[...].reshape(NG * PAD, 128)
    sn_s[:, 0] = dot_tn(emb_g[...].reshape(NG * PAD, COLS), rhs).astype(BF16).reshape(NZ, PAD, 128)
    sn_s[:, 1] = dot_tn(agg_g[...].reshape(NG * PAD, COLS), rhs).astype(BF16).reshape(NZ, PAD, 128)
    scatter_z(sn_s, sn_r, SN_RS)

    got(rbuf2.at[pl.ds(0, DP - 1)], BACK)
    two = dot(sel_t[...], rbuf2[...].reshape(DP * SLOT, 128))
    grad = (own + jnp.concatenate([two[:PAD], two[PAD:]], axis=1)).astype(BF16)
    ng2[0] = grad[:, :128]
    ng2[1] = grad[:, 128:]
    to_columns(ng2, ng_g, NG_G)
    ngrad[...] = grad[:NODE]
    emit(1, ngrad, o_ngrad)

    factor = 1.0 / math.sqrt(NODE * DP)

    def z_total(buf):
        total = buf[0].astype(F32)
        for i in range(1, NZ):
            total = total + buf[i].astype(F32)
        return (total * factor).astype(BF16)

    got(sn_r.at[pl.ds(0, NZ - 1)], SN_RS)
    fin_sn[g, z] = z_total(sn_r)
    gather_z(fin_sn, SN_AG)

    got(pool_g.at[pl.ds(0, NG - 1)], POOL_G)
    got_columns(ng_g, NG_G)
    out = dot_tn(pool_g[...].reshape(NG * PAD, COLS), ng_g[...].reshape(NG * PAD, 128))
    out_s[...] = out.astype(BF16).reshape(NZ, PAD, 128)
    scatter_z(out_s, out_r, OUT_RS)

    got(fin_sn.at[0, pl.ds(0, NZ - 1)], SN_AG)
    y_sends(fin_sn, 0)

    got(out_r.at[pl.ds(0, NZ - 1)], OUT_RS)
    fin_out[g, z] = z_total(out_r)
    gather_z(fin_out, OUT_AG)

    def forward(fin, first):
        for i in range(1, NY):
            at = ((y + NY - i) % NY) * 2 + c
            y_copy(fin, at, y, first + i - 1).wait_recv()
            copy = c_copy(fin, at, (first // 3) * 4 + i)
            copy.start()
            pending.append(copy.wait_send)

    forward(fin_sn, 0)
    got(fin_out.at[0, pl.ds(0, NZ - 1)], OUT_AG)
    y_sends(fin_out, 3)

    for i in range(NY):
        c_copy(fin_sn, ((y + NY - i) % NY) * 2 + 1 - c, i).wait_recv()
    emit(2, fin_sn, o_sn)

    forward(fin_out, 3)
    for i in range(NY):
        c_copy(fin_out, ((y + NY - i) % NY) * 2 + 1 - c, 4 + i).wait_recv()
    emit(3, fin_out, o_out)

    for wait in pending:
        wait()


def step(texts, w_qkv, w_out, w_self, w_neigh, ids, cot):
    anywhere = pl.BlockSpec(memory_space=pl.ANY)
    b, f = (lambda *shape: pltpu.VMEM(shape, BF16)), (lambda *shape: pltpu.VMEM(shape, F32))
    blocks = b(DP, SLOT, 128)
    return pl.pallas_call(
        step_kernel,
        out_shape=[
            jax.ShapeDtypeStruct((NODE, COLS), BF16),
            jax.ShapeDtypeStruct((NODE, COLS), BF16),
            jax.ShapeDtypeStruct((NG, NZ, 2, PAD, 128), BF16),
            jax.ShapeDtypeStruct((NG, NZ, PAD, 128), BF16),
        ],
        in_specs=[anywhere] * 7,
        out_specs=[anywhere] * 4,
        scratch_shapes=[
            b(NODE, COLS),
            b(NODE, COLS),
            b(NG, NZ, 2, PAD, 128),
            b(NG, NZ, PAD, 128),
            b(NODE, 128, WIDTH),
            b(WIDTH, 3 * COLS),
            b(WIDTH, 3 * COLS),
            b(TEXTS * 128, 3 * COLS),
            b(COLS, WIDTH),
            b(COLS, WIDTH),
            b(COLS, WIDTH),
            pltpu.VMEM(ids.shape, jnp.int32),
            b(NODE, COLS),
            f(NODE, COLS),
            f(NODE, COLS),
            b(PAD, COLS),
            blocks,
            b(2 * PAD, DP * SLOT),
            b(DP * SLOT, 128),
            f(PAD, COLS),
            blocks,
            blocks,
            blocks,
            blocks,
            blocks,
            b(2 * PAD, DP * SLOT),
            f(MP, NODE, COLS),
            f(MP, NODE, COLS),
            f(MP, NODE, COLS),
            f(MP, NODE, COLS),
            b(128, 128),
            b(128, 128),
            b(NG, PAD, COLS),
            b(NG, PAD, COLS),
            b(NG, PAD, COLS),
            b(MP, PAD, COLS),
            b(2, PAD, 128),
            b(NG, PAD, 128),
            b(2, PAD, 128),
            b(NG, PAD, 128),
            b(NZ, 2, PAD, 128),
            b(NZ, 2, PAD, 128),
            b(NZ, PAD, 128),
            b(NZ, PAD, 128),
            pltpu.SemaphoreType.DMA((NODE // TEXTS,)),
            pltpu.SemaphoreType.DMA((6,)),
            pltpu.SemaphoreType.DMA((4,)),
            pltpu.SemaphoreType.DMA((15,)),
            pltpu.SemaphoreType.DMA((15,)),
            pltpu.SemaphoreType.DMA((6,)),
            pltpu.SemaphoreType.DMA((6,)),
            pltpu.SemaphoreType.DMA((8,)),
            pltpu.SemaphoreType.DMA((8,)),
        ],
        compiler_params=pltpu.CompilerParams(
            collective_id=0, has_side_effects=True, vmem_limit_bytes=VMEM_LIMIT
        ),
        cost_estimate=pl.CostEstimate(flops=7 * 10**9, bytes_accessed=12 * 10**6, transcendentals=1600000),
    )(texts, w_qkv, w_out, w_self, w_neigh, ids, cot)


def finish_kernel(mixed, ngrad, sn, out, o_mixed, o_ngrad, o_self, o_neigh, o_out, small, fin_sn, fin_out, wide, isem, sem):
    loads = [
        pltpu.make_async_copy(src, dst, isem.at[k])
        for k, (src, dst) in enumerate([(sn, fin_sn), (out, fin_out), (mixed, small.at[0]), (ngrad, small.at[1])])
    ]
    for copy in loads:
        copy.start()
    stores = []

    def store(k, src, dst):
        copy = pltpu.make_async_copy(src, dst, sem.at[k])
        copy.start()
        stores.append(copy)

    for k, dst in enumerate((o_self, o_neigh, o_out)):
        if k != 1:
            loads[k // 2].wait()
        for j in range(NG):
            block = fin_sn[j, :, k] if k < 2 else fin_out[j]
            wide[k, :, j * 128 : j * 128 + 128] = block.reshape(COLS, 128).astype(F32)
        store(k, wide.at[k], dst)
    for k, dst in enumerate((o_mixed, o_ngrad)):
        loads[2 + k].wait()
        store(3 + k, small.at[k], dst)
    for copy in stores:
        copy.wait()


def finish(mixed, ngrad, fin_sn, fin_out):
    anywhere = pl.BlockSpec(memory_space=pl.ANY)
    return pl.pallas_call(
        finish_kernel,
        out_shape=[
            jax.ShapeDtypeStruct((NODE, COLS), BF16),
            jax.ShapeDtypeStruct((NODE, COLS), BF16),
            jax.ShapeDtypeStruct((COLS, WIDTH), F32),
            jax.ShapeDtypeStruct((COLS, WIDTH), F32),
            jax.ShapeDtypeStruct((COLS, WIDTH), F32),
        ],
        in_specs=[anywhere] * 4,
        out_specs=[anywhere] * 5,
        scratch_shapes=[
            pltpu.VMEM((2, NODE, COLS), BF16),
            pltpu.VMEM((NG, NZ, 2, PAD, 128), BF16),
            pltpu.VMEM((NG, NZ, PAD, 128), BF16),
            pltpu.VMEM((3, COLS, WIDTH), F32),
            pltpu.SemaphoreType.DMA((4,)),
            pltpu.SemaphoreType.DMA((5,)),
        ],
        compiler_params=pltpu.CompilerParams(vmem_limit_bytes=VMEM_LIMIT),
        cost_estimate=pl.CostEstimate(flops=0, bytes_accessed=5 * 10**6, transcendentals=0),
    )(mixed, ngrad, fin_sn, fin_out)


def per_device(texts, w_qkv, w_out, w_self, w_neigh, neighbours, cotangent):
    return tuple(finish(*step(texts, w_qkv, w_out, w_self, w_neigh, neighbours.T, cotangent)))


def solution(mesh):
    return jax.shard_map(
        per_device,
        mesh=mesh,
        in_specs=(
            P("dp", None, None),
            P(None, "mp"),
            P("mp", None),
            P("mp", None),
            P("mp", None),
            P("dp", None),
            P("dp", "mp"),
        ),
        out_specs=(P("dp", "mp"), P("dp", "mp"), P("mp", None), P("mp", None), P("mp", None)),
        check_vma=False,
    )
```

time: 104 us -> 78 us (0.75)
  Pallas kernels: 94.4 us -> 77.2 us
  local copies, waits for them, and re-layouts: 9.09 us -> 0 us
    pallas_call x2, Pallas kernels: 94.4 us -> 77.2 us  [the longest x1 74.1 us: step(): pl.pallas_call(step_kernel, out_shape=[jax.ShapeDtypeStruct((NODE, COLS),...]
    unnamed x18 -> x0, local copies, waits for them, and re-layouts: 9.09 us -> none
where the time goes in v2:
time: 78 us; the launch traced here: 77.9 us
  Pallas kernels  77.2 us (99%)
    pallas_call x1, Pallas kernels, step(): pl.pallas_call(step_kernel, out_shape=[jax.ShapeDtypeStruct((NODE, COLS),...  74.1 us
    pallas_call x1, Pallas kernels, finish(): pl.pallas_call(finish_kernel, out_shape=[jax.ShapeDtypeStruct((NODE, COLS...  3.1 us

profile of v2, /device:TPU:1, one launch (start us, length us, event | category | flops | bytes accessed | tf_op | source)
XLA Modules:
  0.0 77.9 jit_solution(3185007877986151515)
XLA Ops:
  0.6 74.1 %shard_map.110 = (bf16[24,256]{1,0:T(8,128)(2,1)}, bf16[24,256]{1,0:T(8,128)(2,1)}, bf16[8,8,2,32,128]{4,3,2,1,0:T(8,128)(2,1)}, bf16[8,8,32,128]{3,2,1,0:T(8,128)(2,1)}) custom-call(bf16[24,128,1024]{2,1,0:T(8,128)(2,1)} %texts_in.1, bf16[1024,768]{1,0:T(8,128)(2,1)} %qkv_in.1, bf16[256,1024]{1,0:T(8,128)(2,1)} %out_in.1, bf16[256,1024]{1,0:T(8,128)(2,1)} %self_in.1, ...), custom_call_target="tpu_custom_call" | custom-call | flops 7000000000 | bytes 12000000 | tf_op jit(solution)/shard_map/pallas_call | solution.py:450
  74.8 3.1 %shard_map.111 = (bf16[24,256]{1,0:T(8,128)(2,1)}, bf16[24,256]{1,0:T(8,128)(2,1)}, f32[256,1024]{1,0:T(8,128)}, f32[256,1024]{1,0:T(8,128)}, f32[256,1024]{1,0:T(8,128)}) custom-call(bf16[24,256]{1,0:T(8,128)(2,1)} %get-tuple-element.9.mixed, bf16[24,256]{1,0:T(8,128)(2,1)} %get-tuple-element.10.ngrad, bf16[8,8,2,32,128]{4,3,2,1,0:T(8,128)(2,1)} %get-tuple-element.11.sn, ...), custom_call_target="tpu_custom_call" | custom-call | bytes 5000000 | tf_op jit(solution)/shard_map/pallas_call | solution.py:552

commit v3 on v2

--- a/solution.py
+++ b/solution.py
@@ -16,6 +16,7 @@
 COLS, WIDTH = 256, 1024
 SLOT = 16
 EMPTY = 120.0
+FAR_FIRST = (4, 3, 5, 2, 6, 1, 7, 0)
 VMEM_LIMIT = 60 * 2**20
 TEXTS = 8
 
@@ -117,16 +118,17 @@
     return jnp.concatenate(texts, axis=0) * (1.0 / 128)
 
 
-ASK, POOL_SUM, ROWS, EMB_G, POOL_G, AGG_G, Z_SUM, DZ, DZ_G, BACK, NG_G, SN_RS, SN_AG, OUT_RS, OUT_AG = range(15)
+ASK, POOL_SUM, ROWS, POOL_ROWS, EMB_G, POOL_G, AGG_G, AGP_G, Z_ALL, COT, DZ_G, BACK, FACT = range(13)
+SN_RS, OUT_RS = range(13, 15)
 
 
 def step_kernel(
     texts_in, qkv_in, out_in, self_in, neigh_in, ids_in, cot_in,
     o_mixed, o_ngrad, o_sn, o_out,
     mixed, ngrad, fin_sn, fin_out, tx, wq, wp, qkv, w_out, w_self, w_neigh, ids, cot, acc, tmean, pooled, want, gh, ght, cnt,
-    asked, sbuf, rbuf, sbuf2, rbuf2, sel_t, part, sums, zpart, zsums, e2, m2,
-    emb_g, pool_g, agg_g, dzf, dz2, dz_g, ng2, ng_g, sn_s, sn_r, out_s, out_r,
-    tsem, lsem, osem, ssem, rsem, y_s, y_r, c_s, c_r,
+    asked, sel, sbufp, rbufp, sbuf, rbuf, sbuf2, rbuf2, sel_t, part, sums, cots, zsend, zall, full, e2, m2,
+    emb_g, pool_g, agg_g, agp_g, dz2, dz_g, fact, fact_g, sn_s, sn_r, out_s, out_r,
+    tsem, lsem, osem, ssem, rsem, z_s, z_r, y_s, y_r, c_s, c_r,
 ):
     m, d = lax.axis_index("mp"), lax.axis_index("dp")
     z, g = d // NG, d % NG
@@ -162,8 +164,8 @@
 
         lax.fori_loop(1, count, step, 0)
 
-    def to_dp(src, dst, phase):
-        for k in (4, 3, 5, 2, 6, 1, 7, 0):
+    def to_dp(src, dst, phase, offsets=FAR_FIRST):
+        for k in offsets:
 
             def one(i, carry):
                 to = ((z + k) % NZ) * NG + (g + i) % NG
@@ -171,8 +173,9 @@
                 return carry
 
             lax.fori_loop(1 if k == 0 else 0, NG, one, 0)
-        dst[d] = src[d]
-        later(dst.at[pl.ds(0, DP - 1)], phase)
+        if offsets[-1] == 0:
+            dst[d] = src[d]
+            later(dst.at[pl.ds(0, DP - 1)], phase)
 
     def to_mp(src, dst, phase):
         for i in range(1, MP):
@@ -181,6 +184,11 @@
         dst[m] = src[m]
         later(dst.at[pl.ds(0, MP - 1)], phase)
 
+    def share_mp(src, dst, phase):
+        for i in range(1, MP):
+            send(src, dst.at[m], phase, d, (m + i) % MP)
+        later(dst.at[pl.ds(0, MP - 1)], phase)
+
     def to_group(block, phase):
         for i in range(1, NG):
             send(block.at[g], block.at[g], phase, z * NG + (g + i) % NG, m)
@@ -230,32 +238,54 @@
         dst[z] = src[z]
         later(dst.at[pl.ds(0, NZ - 1)], phase)
 
-    def gather_z(fin, phase):
-        for i in range(1, NZ):
-            to = (z + i) % NZ
-            send(fin.at[g, z], fin.at[g, z], phase, to * NG + g, m)
-        later(fin.at[0, pl.ds(0, NZ - 1)], phase)
-
-    def y_copy(fin, at, to, k):
+    def z_copy(fin, at, to, k, which):
         return pltpu.make_async_remote_copy(
-            src_ref=fin.at[at], dst_ref=fin.at[at], send_sem=y_s.at[k], recv_sem=y_r.at[k],
-            device_id=(z * NG + to * 2 + c, m), device_id_type=MESH,
+            src_ref=fin.at[g, at], dst_ref=fin.at[g, at], send_sem=z_s.at[which, k], recv_sem=z_r.at[which, k],
+            device_id=(to * NG + g, m), device_id_type=MESH,
         )
 
-    def c_copy(fin, at, k):
+    def along_y(fin, at, which):
+        for i in range(1, NY):
+            pltpu.make_async_remote_copy(
+                src_ref=fin.at[g, at], dst_ref=fin.at[g, at], send_sem=y_s.at[which, i], recv_sem=y_r.at[which, i],
+                device_id=(z * NG + ((y + i) % NY) * 2 + c, m), device_id_type=MESH,
+            ).start()
+
+    def c_copy(fin, at, k, which):
         return pltpu.make_async_remote_copy(
-            src_ref=fin.at[at], dst_ref=fin.at[at], send_sem=c_s.at[k], recv_sem=c_r.at[k],
+            src_ref=fin.at[at], dst_ref=fin.at[at], send_sem=c_s.at[which, k], recv_sem=c_r.at[which, k],
             device_id=(z * NG + y * 2 + 1 - c, m), device_id_type=MESH,
         )
 
-    def y_sends(fin, first):
-        for i in range(1, NY):
-            copy = y_copy(fin, g, (y + i) % NY, first + i - 1)
+    def start_gather(fin, which):
+        for k in FAR_FIRST[:-1]:
+            copy = z_copy(fin, z, (z + k) % NZ, k, which)
             copy.start()
             pending.append(copy.wait_send)
-        own = c_copy(fin, g, (first // 3) * 4)
+        along_y(fin, z, which)
+
+    def pass_along_y(fin, which):
+        for k in reversed(FAR_FIRST[:-1]):
+            at = (z + NZ - k) % NZ
+            z_copy(fin, at, z, k, which).wait_recv()
+            along_y(fin, at, which)
+        own = c_copy(fin, g, 0, which)
         own.start()
         pending.append(own.wait_send)
+        for i in range(1, NY):
+            pending.append(pltpu.make_async_copy(fin.at[g], fin.at[g], y_s.at[which, i]).wait)
+
+    def pass_to_core(fin, which):
+        for i in range(1, NY):
+            at = ((y + NY - i) % NY) * 2 + c
+            pltpu.make_async_copy(fin.at[at], fin.at[at], y_r.at[which, i]).wait()
+            copy = c_copy(fin, at, i, which)
+            copy.start()
+            pending.append(copy.wait_send)
+
+    def end_gather(fin, which):
+        for i in range(NY):
+            c_copy(fin, ((y + NY - i) % NY) * 2 + 1 - c, i, which).wait_recv()
 
     weight = pltpu.make_async_copy(qkv_in, wq, lsem.at[0])
     names_in = pltpu.make_async_copy(ids_in, ids, lsem.at[1])
@@ -298,8 +328,6 @@
     m2[...] = jnp.zeros_like(m2)
     weight.wait()
     order_columns(wq, wp)
-    pl.semaphore_wait(bar, DP - 1 + MP - 1 + 2 * MP - is_diag.astype(jnp.int32))
-    to_dp(want, asked, ASK)
 
     def work(i, carry):
         chunk(i).wait()
@@ -308,6 +336,12 @@
         acc[rows, :] = attend(qkv)
         mine = tx[rows, :, pl.ds(pl.multiple_of(m * COLS, COLS), COLS)]
         tmean[rows, :] = jnp.sum(mine.astype(F32), axis=1) * (1.0 / 128)
+
+        @pl.when(i == 0)
+        def _():
+            pl.semaphore_wait(bar, DP - 1 + MP - 1 + 2 * MP - is_diag.astype(jnp.int32))
+            to_dp(want, asked, ASK)
+
         return carry
 
     lax.fori_loop(0, chunks, work, 0)
@@ -319,79 +353,94 @@
     for j in range(MP):
         part[j] = first[:NODE, j * COLS : (j + 1) * COLS]
 
+    def halves(dst, x):
+        dst[0:PAD, :] = x[:, :128]
+        dst[PAD : 2 * PAD, :] = x[:, 128:]
+
+    def whole(x):
+        return jnp.concatenate([x[:PAD], x[PAD : 2 * PAD]], axis=1)
+
+    def rows_of(onehot, x):
+        return dot(onehot, x).astype(BF16).reshape(DP, SLOT, 128)
+
     to_mp(part, sums, POOL_SUM)
+    cots[m] = pad_rows(cot[...], PAD)
+    share_mp(cots.at[m], cots, COT)
+    got(asked.at[pl.ds(0, DP - 1)], ASK)
+    names = asked[...].reshape(DP * SLOT, 128).astype(F32)
+    hot = (names == iota((DP * SLOT, 128), 1).astype(F32)).astype(F32)
+    sel[...] = hot.astype(BF16)
+    halves(m2, pooled[...])
+    sbufp[...] = rows_of(sel[...], m2[...])
+    sel_t[...] = jnp.transpose(hot)[: 2 * PAD].astype(BF16)
     got(sums.at[pl.ds(0, MP - 1)], POOL_SUM)
     embed = tmean[...] + (sums[0] + sums[1] + sums[2] + sums[3])
     embed = pad_rows(embed, PAD).astype(BF16)
-    e2[0:PAD, :] = embed[:, :128]
-    e2[PAD : 2 * PAD, :] = embed[:, 128:]
+    halves(e2, embed)
     emb_g[g] = embed
 
-    got(asked.at[pl.ds(0, DP - 1)], ASK)
-    names = asked[...].reshape(DP * SLOT, 128).astype(F32)
-    sel = (names == iota((DP * SLOT, 128), 1).astype(F32)).astype(F32)
-    sbuf[...] = dot(sel.astype(BF16), e2[...]).astype(BF16).reshape(DP, SLOT, 128)
+    sbuf[...] = rows_of(sel[...], e2[...])
     to_dp(sbuf, rbuf, ROWS)
+    to_dp(sbufp, rbufp, POOL_ROWS)
+    zself = dot(embed, w_self[...])
     to_group(emb_g, EMB_G)
     to_group(pool_g, POOL_G)
-    sel_t[...] = jnp.transpose(sel)[: 2 * PAD].astype(BF16)
-    zself = dot(embed, w_self[...])
     got(rbuf.at[pl.ds(0, DP - 1)], ROWS)
-    two = dot(gh[...], rbuf[...].reshape(DP * SLOT, 128))
-    agg = (jnp.concatenate([two[:PAD], two[PAD:]], axis=1) / cnt[...]).astype(BF16)
+    agg = (whole(dot(gh[...], rbuf[...].reshape(DP * SLOT, 128))) / cnt[...]).astype(BF16)
     zfull = zself + dot(agg, w_neigh[...])
-    for j in range(MP):
-        zpart[j] = zfull[:NODE, j * COLS : (j + 1) * COLS]
-    to_mp(zpart, zsums, Z_SUM)
+    zsend[...] = zfull.astype(BF16)
+    share_mp(zsend, zall, Z_ALL)
+    zall[m] = jnp.zeros((PAD, WIDTH), BF16)
     agg_g[g] = agg
     to_group(agg_g, AGG_G)
-    got(zsums.at[pl.ds(0, MP - 1)], Z_SUM)
-    zc = zsums[0] + zsums[1] + zsums[2] + zsums[3]
+    got(cots.at[pl.ds(0, MP - 1)], COT)
+    got(zall.at[pl.ds(0, MP - 1)], Z_ALL)
+    zc = zfull
+    for j in range(MP):
+        zc = zc + zall[j].astype(F32)
 
     root = math.sqrt(2.0 / math.pi)
     th = jnp.tanh(root * (zc + 0.044715 * (zc * zc * zc)))
     cdf = 0.5 * (1.0 + th)
     slope = cdf + zc * (0.5 * (1.0 - th * th) * (root * (1.0 + (3 * 0.044715) * (zc * zc))))
-    dz = pad_rows(cot[...].astype(F32) * slope, PAD).astype(BF16)
-    dzf[m] = dz
-    for i in range(1, MP):
-        send(dzf.at[m], dzf.at[m], DZ, d, (m + i) % MP)
-    later(dzf.at[pl.ds(0, MP - 1)], DZ)
-    dz2[0] = dz[:, :128]
-    dz2[1] = dz[:, 128:]
-    to_columns(dz2, dz_g, DZ_G)
-    mixed[...] = (zc * cdf).astype(BF16)
+    dz = (jnp.concatenate([cots[j] for j in range(MP)], axis=1).astype(F32) * slope).astype(BF16)
+    for j in range(NG):
+        dz2[j] = dz[:, j * 128 : j * 128 + 128]
+    for i in range(1, NG):
+        to = (g + i) % NG
+        send(dz2.at[to], dz_g.at[g], DZ_G, z * NG + to, m)
+    dz_g[g] = dz2[g]
+    later(dz_g.at[pl.ds(0, NG - 1)], DZ_G)
+
+    own = dot_nt(dz, w_self[...])
+    msg = (dot_nt(dz, w_neigh[...]) / cnt[...]).astype(BF16)
+    for k, x in enumerate((own.astype(BF16), msg)):
+        fact[0, k] = x[:, :128]
+        fact[1, k] = x[:, 128:]
+    to_columns(fact, fact_g, FACT)
+    full[...] = zc * cdf
+    mixed[...] = full[:NODE, pl.ds(pl.multiple_of(m * COLS, COLS), COLS)].astype(BF16)
     emit(0, mixed, o_mixed)
-    got(dzf.at[pl.ds(0, MP - 1)], DZ)
-
-    dagg = dot_nt(dzf[0], w_neigh[:, 0:COLS])
-    for j in range(1, MP):
-        dagg = dagg + dot_nt(dzf[j], w_neigh[:, j * COLS : (j + 1) * COLS])
-    msg = (dagg / cnt[...]).astype(BF16)
-    m2[0:PAD, :] = msg[:, :128]
-    m2[PAD : 2 * PAD, :] = msg[:, 128:]
-    sbuf2[...] = dot(ght[...], m2[...]).astype(BF16).reshape(DP, SLOT, 128)
-    to_dp(sbuf2, rbuf2, BACK)
-    own = dot_nt(dzf[0], w_self[:, 0:COLS])
-    for j in range(1, MP):
-        own = own + dot_nt(dzf[j], w_self[:, j * COLS : (j + 1) * COLS])
-
-    got_columns(dz_g, DZ_G)
+
+    def grad_of(lhs, rhs):
+        return dot_tn(lhs[...].reshape(NG * PAD, COLS), rhs.reshape(NG * PAD, 128))
+
+    def rounded(x):
+        return x.astype(BF16).reshape(NZ, PAD, 128)
+
+    got(dz_g.at[pl.ds(0, NG - 1)], DZ_G)
     got(emb_g.at[pl.ds(0, NG - 1)], EMB_G)
     got(agg_g.at[pl.ds(0, NG - 1)], AGG_G)
-    rhs = dz_g[...].reshape(NG * PAD, 128)
-    sn_s[:, 0] = dot_tn(emb_g[...].reshape(NG * PAD, COLS), rhs).astype(BF16).reshape(NZ, PAD, 128)
-    sn_s[:, 1] = dot_tn(agg_g[...].reshape(NG * PAD, COLS), rhs).astype(BF16).reshape(NZ, PAD, 128)
+    sn_s[:, 0] = rounded(grad_of(emb_g, dz_g[...]))
+    sn_s[:, 1] = rounded(grad_of(agg_g, dz_g[...]))
     scatter_z(sn_s, sn_r, SN_RS)
 
-    got(rbuf2.at[pl.ds(0, DP - 1)], BACK)
-    two = dot(sel_t[...], rbuf2[...].reshape(DP * SLOT, 128))
-    grad = (own + jnp.concatenate([two[:PAD], two[PAD:]], axis=1)).astype(BF16)
-    ng2[0] = grad[:, :128]
-    ng2[1] = grad[:, 128:]
-    to_columns(ng2, ng_g, NG_G)
-    ngrad[...] = grad[:NODE]
-    emit(1, ngrad, o_ngrad)
+    got(rbufp.at[pl.ds(0, DP - 1)], POOL_ROWS)
+    agp_g[g] = whole(dot(gh[...], rbufp[...].reshape(DP * SLOT, 128))).astype(BF16)
+    to_group(agp_g, AGP_G)
+
+    halves(m2, msg)
+    sbuf2[...] = rows_of(ght[...], m2[...])
 
     factor = 1.0 / math.sqrt(NODE * DP)
 
@@ -401,42 +450,31 @@
             total = total + buf[i].astype(F32)
         return (total * factor).astype(BF16)
 
+    got(pool_g.at[pl.ds(0, NG - 1)], POOL_G)
+    got(agp_g.at[pl.ds(0, NG - 1)], AGP_G)
+    got_columns(fact_g, FACT)
+    out_s[...] = rounded(grad_of(pool_g, fact_g[:, 0]) + grad_of(agp_g, fact_g[:, 1]))
+    scatter_z(out_s, out_r, OUT_RS)
     got(sn_r.at[pl.ds(0, NZ - 1)], SN_RS)
     fin_sn[g, z] = z_total(sn_r)
-    gather_z(fin_sn, SN_AG)
-
-    got(pool_g.at[pl.ds(0, NG - 1)], POOL_G)
-    got_columns(ng_g, NG_G)
-    out = dot_tn(pool_g[...].reshape(NG * PAD, COLS), ng_g[...].reshape(NG * PAD, 128))
-    out_s[...] = out.astype(BF16).reshape(NZ, PAD, 128)
-    scatter_z(out_s, out_r, OUT_RS)
-
-    got(fin_sn.at[0, pl.ds(0, NZ - 1)], SN_AG)
-    y_sends(fin_sn, 0)
+    start_gather(fin_sn, 0)
 
     got(out_r.at[pl.ds(0, NZ - 1)], OUT_RS)
     fin_out[g, z] = z_total(out_r)
-    gather_z(fin_out, OUT_AG)
-
-    def forward(fin, first):
-        for i in range(1, NY):
-            at = ((y + NY - i) % NY) * 2 + c
-            y_copy(fin, at, y, first + i - 1).wait_recv()
-            copy = c_copy(fin, at, (first // 3) * 4 + i)
-            copy.start()
-            pending.append(copy.wait_send)
-
-    forward(fin_sn, 0)
-    got(fin_out.at[0, pl.ds(0, NZ - 1)], OUT_AG)
-    y_sends(fin_out, 3)
-
-    for i in range(NY):
-        c_copy(fin_sn, ((y + NY - i) % NY) * 2 + 1 - c, i).wait_recv()
+    start_gather(fin_out, 1)
+    pass_along_y(fin_sn, 0)
+    to_dp(sbuf2, rbuf2, BACK)
+    pass_along_y(fin_out, 1)
+    pass_to_core(fin_sn, 0)
+
+    got(rbuf2.at[pl.ds(0, DP - 1)], BACK)
+    grad = own + whole(dot(sel_t[...], rbuf2[...].reshape(DP * SLOT, 128)))
+    ngrad[...] = grad[:NODE].astype(BF16)
+    emit(1, ngrad, o_ngrad)
+    end_gather(fin_sn, 0)
     emit(2, fin_sn, o_sn)
-
-    forward(fin_out, 3)
-    for i in range(NY):
-        c_copy(fin_out, ((y + NY - i) % NY) * 2 + 1 - c, 4 + i).wait_recv()
+    pass_to_core(fin_out, 1)
+    end_gather(fin_out, 1)
     emit(3, fin_out, o_out)
 
     for wait in pending:
@@ -479,6 +517,9 @@
             b(DP * SLOT, 128),
             f(PAD, COLS),
             blocks,
+            b(DP * SLOT, 128),
+            blocks,
+            blocks,
             blocks,
             blocks,
             blocks,
@@ -486,18 +527,20 @@
             b(2 * PAD, DP * SLOT),
             f(MP, NODE, COLS),
             f(MP, NODE, COLS),
-            f(MP, NODE, COLS),
-            f(MP, NODE, COLS),
+            b(MP, PAD, COLS),
+            b(PAD, WIDTH),
+            b(MP, PAD, WIDTH),
+            f(PAD, WIDTH),
             b(128, 128),
             b(128, 128),
             b(NG, PAD, COLS),
             b(NG, PAD, COLS),
             b(NG, PAD, COLS),
-            b(MP, PAD, COLS),
-            b(2, PAD, 128),
+            b(NG, PAD, COLS),
             b(NG, PAD, 128),
-            b(2, PAD, 128),
             b(NG, PAD, 128),
+            b(2, 2, PAD, 128),
+            b(NG, 2, PAD, 128),
             b(NZ, 2, PAD, 128),
             b(NZ, 2, PAD, 128),
             b(NZ, PAD, 128),
@@ -507,10 +550,12 @@
             pltpu.SemaphoreType.DMA((4,)),
             pltpu.SemaphoreType.DMA((15,)),
             pltpu.SemaphoreType.DMA((15,)),
-            pltpu.SemaphoreType.DMA((6,)),
-            pltpu.SemaphoreType.DMA((6,)),
-            pltpu.SemaphoreType.DMA((8,)),
-            pltpu.SemaphoreType.DMA((8,)),
+            pltpu.SemaphoreType.DMA((2, NZ)),
+            pltpu.SemaphoreType.DMA((2, NZ)),
+            pltpu.SemaphoreType.DMA((2, NY)),
+            pltpu.SemaphoreType.DMA((2, NY)),
+            pltpu.SemaphoreType.DMA((2, NY)),
+            pltpu.SemaphoreType.DMA((2, NY)),
         ],
         compiler_params=pltpu.CompilerParams(
             collective_id=0, has_side_effects=True, vmem_limit_bytes=VMEM_LIMIT

time: 78 us -> 74.3 us (0.953)
  Pallas kernels: 77.2 us -> 73.6 us
    pallas_call x1, Pallas kernels: 74.1 us -> 70.5 us  [step(): pl.pallas_call(step_kernel, out_shape=[jax.ShapeDtypeStruct((NODE, COLS),...]
where the time goes in v3:
time: 74.3 us; the launch traced here: 74.2 us
  Pallas kernels  73.6 us (99%)
    pallas_call x1, Pallas kernels, step(): pl.pallas_call(step_kernel, out_shape=[jax.ShapeDtypeStruct((NODE, COLS),...  70.5 us
    pallas_call x1, Pallas kernels, finish(): pl.pallas_call(finish_kernel, out_shape=[jax.ShapeDtypeStruct((NODE, COLS...  3.1 us

profile of v3, /device:TPU:1, one launch (start us, length us, event | category | flops | bytes accessed | tf_op | source)
XLA Modules:
  0.0 74.2 jit_solution(13146738342384615166)
XLA Ops:
  0.6 70.5 %shard_map.110 = (bf16[24,256]{1,0:T(8,128)(2,1)}, bf16[24,256]{1,0:T(8,128)(2,1)}, bf16[8,8,2,32,128]{4,3,2,1,0:T(8,128)(2,1)}, bf16[8,8,32,128]{3,2,1,0:T(8,128)(2,1)}) custom-call(bf16[24,128,1024]{2,1,0:T(8,128)(2,1)} %texts_in.1, bf16[1024,768]{1,0:T(8,128)(2,1)} %qkv_in.1, bf16[256,1024]{1,0:T(8,128)(2,1)} %out_in.1, bf16[256,1024]{1,0:T(8,128)(2,1)} %self_in.1, ...), custom_call_target="tpu_custom_call" | custom-call | flops 7000000000 | bytes 12000000 | tf_op jit(solution)/shard_map/pallas_call | solution.py:488
  71.1 3.1 %shard_map.111 = (bf16[24,256]{1,0:T(8,128)(2,1)}, bf16[24,256]{1,0:T(8,128)(2,1)}, f32[256,1024]{1,0:T(8,128)}, f32[256,1024]{1,0:T(8,128)}, f32[256,1024]{1,0:T(8,128)}) custom-call(bf16[24,256]{1,0:T(8,128)(2,1)} %get-tuple-element.9.mixed, bf16[24,256]{1,0:T(8,128)(2,1)} %get-tuple-element.10.ngrad, bf16[8,8,2,32,128]{4,3,2,1,0:T(8,128)(2,1)} %get-tuple-element.11.sn, ...), custom_call_target="tpu_custom_call" | custom-call | bytes 5000000 | tf_op jit(solution)/shard_map/pallas_call | solution.py:597

commit v4 on v3

--- a/solution.py
+++ b/solution.py
@@ -388,16 +388,22 @@
     got(rbuf.at[pl.ds(0, DP - 1)], ROWS)
     agg = (whole(dot(gh[...], rbuf[...].reshape(DP * SLOT, 128))) / cnt[...]).astype(BF16)
     zfull = zself + dot(agg, w_neigh[...])
-    zsend[...] = zfull.astype(BF16)
+    zsend[...] = jnp.concatenate([zfull[:NODE, : WIDTH // 2], zfull[:NODE, WIDTH // 2 :]], axis=0).astype(BF16)
     share_mp(zsend, zall, Z_ALL)
-    zall[m] = jnp.zeros((PAD, WIDTH), BF16)
+    zall[m] = jnp.zeros((2 * NODE, WIDTH // 2), BF16)
     agg_g[g] = agg
     to_group(agg_g, AGG_G)
+    got(rbufp.at[pl.ds(0, DP - 1)], POOL_ROWS)
+    agp_g[g] = whole(dot(gh[...], rbufp[...].reshape(DP * SLOT, 128))).astype(BF16)
+    to_group(agp_g, AGP_G)
+
+
     got(cots.at[pl.ds(0, MP - 1)], COT)
     got(zall.at[pl.ds(0, MP - 1)], Z_ALL)
-    zc = zfull
-    for j in range(MP):
-        zc = zc + zall[j].astype(F32)
+    total = zall[0].astype(F32)
+    for j in range(1, MP):
+        total = total + zall[j].astype(F32)
+    zc = zfull + pad_rows(jnp.concatenate([total[:NODE], total[NODE:]], axis=1), PAD)
 
     root = math.sqrt(2.0 / math.pi)
     th = jnp.tanh(root * (zc + 0.044715 * (zc * zc * zc)))
@@ -418,6 +424,9 @@
         fact[0, k] = x[:, :128]
         fact[1, k] = x[:, 128:]
     to_columns(fact, fact_g, FACT)
+    halves(m2, msg)
+    sbuf2[...] = rows_of(ght[...], m2[...])
+    to_dp(sbuf2, rbuf2, BACK)
     full[...] = zc * cdf
     mixed[...] = full[:NODE, pl.ds(pl.multiple_of(m * COLS, COLS), COLS)].astype(BF16)
     emit(0, mixed, o_mixed)
@@ -434,13 +443,6 @@
     sn_s[:, 0] = rounded(grad_of(emb_g, dz_g[...]))
     sn_s[:, 1] = rounded(grad_of(agg_g, dz_g[...]))
     scatter_z(sn_s, sn_r, SN_RS)
-
-    got(rbufp.at[pl.ds(0, DP - 1)], POOL_ROWS)
-    agp_g[g] = whole(dot(gh[...], rbufp[...].reshape(DP * SLOT, 128))).astype(BF16)
-    to_group(agp_g, AGP_G)
-
-    halves(m2, msg)
-    sbuf2[...] = rows_of(ght[...], m2[...])
 
     factor = 1.0 / math.sqrt(NODE * DP)
 
@@ -463,7 +465,6 @@
     fin_out[g, z] = z_total(out_r)
     start_gather(fin_out, 1)
     pass_along_y(fin_sn, 0)
-    to_dp(sbuf2, rbuf2, BACK)
     pass_along_y(fin_out, 1)
     pass_to_core(fin_sn, 0)
 
@@ -528,8 +529,8 @@
             f(MP, NODE, COLS),
             f(MP, NODE, COLS),
             b(MP, PAD, COLS),
-            b(PAD, WIDTH),
-            b(MP, PAD, WIDTH),
+            b(2 * NODE, WIDTH // 2),
+            b(MP, 2 * NODE, WIDTH // 2),
             f(PAD, WIDTH),
             b(128, 128),
             b(128, 128),
@@ -565,29 +566,32 @@
 
 
 def finish_kernel(mixed, ngrad, sn, out, o_mixed, o_ngrad, o_self, o_neigh, o_out, small, fin_sn, fin_out, wide, isem, sem):
-    loads = [
-        pltpu.make_async_copy(src, dst, isem.at[k])
-        for k, (src, dst) in enumerate([(sn, fin_sn), (out, fin_out), (mixed, small.at[0]), (ngrad, small.at[1])])
-    ]
-    for copy in loads:
+    def load(k, src, dst):
+        copy = pltpu.make_async_copy(src, dst, isem.at[k])
         copy.start()
-    stores = []
+        return copy
 
     def store(k, src, dst):
         copy = pltpu.make_async_copy(src, dst, sem.at[k])
         copy.start()
-        stores.append(copy)
-
-    for k, dst in enumerate((o_self, o_neigh, o_out)):
-        if k != 1:
-            loads[k // 2].wait()
-        for j in range(NG):
+        return copy
+
+    blocks = [
+        (load(j, sn.at[j], fin_sn.at[j]), load(NG + j, out.at[j], fin_out.at[j])) for j in range(NG)
+    ]
+    loads = [load(2 * NG + k, src, small.at[k]) for k, src in enumerate((mixed, ngrad))]
+    stores = []
+    for j in range(NG):
+        cols = pl.ds(j * 128, 128)
+        for copy in blocks[j]:
+            copy.wait()
+        for k, dst in enumerate((o_self, o_neigh, o_out)):
             block = fin_sn[j, :, k] if k < 2 else fin_out[j]
-            wide[k, :, j * 128 : j * 128 + 128] = block.reshape(COLS, 128).astype(F32)
-        store(k, wide.at[k], dst)
+            wide[k, :, cols] = block.reshape(COLS, 128).astype(F32)
+            stores.append(store(3 * j + k, wide.at[k, :, cols], dst.at[:, cols]))
     for k, dst in enumerate((o_mixed, o_ngrad)):
-        loads[2 + k].wait()
-        store(3 + k, small.at[k], dst)
+        loads[k].wait()
+        stores.append(store(3 * NG + k, small.at[k], dst))
     for copy in stores:
         copy.wait()
 
@@ -610,8 +614,8 @@
             pltpu.VMEM((NG, NZ, 2, PAD, 128), BF16),
             pltpu.VMEM((NG, NZ, PAD, 128), BF16),
             pltpu.VMEM((3, COLS, WIDTH), F32),
-            pltpu.SemaphoreType.DMA((4,)),
-            pltpu.SemaphoreType.DMA((5,)),
+            pltpu.SemaphoreType.DMA((2 * NG + 2,)),
+            pltpu.SemaphoreType.DMA((3 * NG + 2,)),
         ],
         compiler_params=pltpu.CompilerParams(vmem_limit_bytes=VMEM_LIMIT),
         cost_estimate=pl.CostEstimate(flops=0, bytes_accessed=5 * 10**6, transcendentals=0),

time: 74.3 us -> 71.8 us (0.966)
  Pallas kernels: 73.6 us -> 71 us
    pallas_call x1, Pallas kernels: 70.5 us -> 68.1 us  [step(): pl.pallas_call(step_kernel, out_shape=[jax.ShapeDtypeStruct((NODE, COLS),...]
where the time goes in v4:
time: 71.8 us; the launch traced here: 71.7 us
  Pallas kernels  71 us (99%)
    pallas_call x1, Pallas kernels, step(): pl.pallas_call(step_kernel, out_shape=[jax.ShapeDtypeStruct((NODE, COLS),...  68.1 us
    pallas_call x1, Pallas kernels, finish(): pl.pallas_call(finish_kernel, out_shape=[jax.ShapeDtypeStruct((NODE, COLS...  2.96 us

profile of v4, /device:TPU:1, one launch (start us, length us, event | category | flops | bytes accessed | tf_op | source)
XLA Modules:
  0.0 71.7 jit_solution(1238628760533103453)
XLA Ops:
  0.6 68.1 %shard_map.110 = (bf16[24,256]{1,0:T(8,128)(2,1)}, bf16[24,256]{1,0:T(8,128)(2,1)}, bf16[8,8,2,32,128]{4,3,2,1,0:T(8,128)(2,1)}, bf16[8,8,32,128]{3,2,1,0:T(8,128)(2,1)}) custom-call(bf16[24,128,1024]{2,1,0:T(8,128)(2,1)} %texts_in.1, bf16[1024,768]{1,0:T(8,128)(2,1)} %qkv_in.1, bf16[256,1024]{1,0:T(8,128)(2,1)} %out_in.1, bf16[256,1024]{1,0:T(8,128)(2,1)} %self_in.1, ...), custom_call_target="tpu_custom_call" | custom-call | flops 7000000000 | bytes 12000000 | tf_op jit(solution)/shard_map/pallas_call | solution.py:489
  68.7 3.0 %shard_map.111 = (bf16[24,256]{1,0:T(8,128)(2,1)}, bf16[24,256]{1,0:T(8,128)(2,1)}, f32[256,1024]{1,0:T(8,128)}, f32[256,1024]{1,0:T(8,128)}, f32[256,1024]{1,0:T(8,128)}) custom-call(bf16[24,256]{1,0:T(8,128)(2,1)} %get-tuple-element.9.mixed, bf16[24,256]{1,0:T(8,128)(2,1)} %get-tuple-element.10.ngrad, bf16[8,8,2,32,128]{4,3,2,1,0:T(8,128)(2,1)} %get-tuple-element.11.sn, ...), custom_call_target="tpu_custom_call" | custom-call | bytes 5000000 | tf_op jit(solution)/shard_map/pallas_call | solution.py:601

commit v5 on v4

--- a/solution.py
+++ b/solution.py
@@ -16,6 +16,8 @@
 COLS, WIDTH = 256, 1024
 SLOT = 16
 EMPTY = 120.0
+MP_ORDER = (2, 1, 3)
+GROUP_ORDER = (4, 5, 3, 2, 6, 7, 1)
 FAR_FIRST = (4, 3, 5, 2, 6, 1, 7, 0)
 VMEM_LIMIT = 60 * 2**20
 TEXTS = 8
@@ -41,15 +43,11 @@
     return jnp.concatenate([x, jnp.zeros((rows - x.shape[0], x.shape[1]), x.dtype)], axis=0)
 
 
-def routing(ids_ref, want, gh, ght, cnt_out):
+def request_names(ids_ref, want, spots_ref):
     ids = jnp.transpose(ids_ref[...].astype(F32))
     own = jnp.floor((ids + 0.5) * (1.0 / NODE))
     loc = ids - NODE * own
     live = ids >= 0.0
-    cnt = jnp.maximum(jnp.sum(live.astype(F32), axis=1, keepdims=True), 1.0)
-    cnt_out[...] = jnp.concatenate(
-        [jnp.broadcast_to(cnt, (NODE, COLS)), jnp.ones((PAD - NODE, COLS), F32)], axis=0
-    )
     fan = ids.shape[1]
     groups = iota((NODE, DP), 1).astype(F32)
     hots = [(own[:, f : f + 1] == groups).astype(F32) for f in range(fan)]
@@ -58,27 +56,35 @@
         total = total + hots[f]
     lower = (iota((NODE, NODE), 1) < iota((NODE, NODE), 0)).astype(BF16)
     run = dot(lower, total.astype(BF16))
+    lanes = iota((NODE, 128), 1).astype(F32)
+    places, asks = [], []
+    for f in range(fan):
+        rank = jnp.sum(hots[f] * run, axis=1, keepdims=True)
+        run = run + hots[f]
+        places.append(jnp.where(live[:, f : f + 1], own[:, f : f + 1] * SLOT + rank, -1000.0))
+        asks.append(jnp.where(lanes == rank, loc[:, f : f + 1] - EMPTY, 0.0))
+    spots_ref[...] = jnp.concatenate(places, axis=1)
+    owners = jnp.concatenate(hots, axis=0).astype(BF16)
+    want[...] = dot_tn(owners, jnp.concatenate(asks, axis=0).astype(BF16)) + EMPTY
+
+
+def routing(spots_ref, gh, ght, cnt_out):
+    at = spots_ref[...]
+    live = (at >= 0.0).astype(F32)
+    cnt = jnp.maximum(jnp.sum(live, axis=1, keepdims=True), 1.0)
+    cnt_out[...] = jnp.concatenate(
+        [jnp.broadcast_to(cnt, (NODE, COLS)), jnp.ones((PAD - NODE, COLS), F32)], axis=0
+    )
     spots = iota((NODE, DP * SLOT), 1).astype(F32)
     left = jnp.zeros((NODE, DP * SLOT), F32)
     right = jnp.zeros((NODE, DP * SLOT), F32)
-    names = jnp.zeros((NODE, DP * SLOT), F32)
-    for f in range(fan):
-        rank = jnp.sum(hots[f] * run, axis=1, keepdims=True)
-        run = run + hots[f]
-        at = jnp.where(live[:, f : f + 1], own[:, f : f + 1] * SLOT + rank, -1000.0)
-        name = loc[:, f : f + 1]
-        is_left = spots == at
-        is_right = spots == at + 8.0
-        left = left + is_left.astype(F32)
-        right = right + is_right.astype(F32)
-        names = names + jnp.where(is_left, name - EMPTY, 0.0)
-        names = names + jnp.where(is_right, name + (PAD - EMPTY), 0.0)
+    for f in range(at.shape[1]):
+        left = jnp.where(spots == at[:, f : f + 1], 1.0, left)
+        right = jnp.where(spots == at[:, f : f + 1] + 8.0, 1.0, right)
     gap = jnp.zeros((PAD - NODE, DP * SLOT), F32)
     both = jnp.concatenate([left, gap, right, gap], axis=0)
     gh[...] = both.astype(BF16)
     ght[...] = jnp.transpose(pad_rows(both, 128)).astype(BF16)
-    spread = jnp.transpose(pad_rows(names, 128)).astype(BF16)
-    want[...] = (dot(spread, jnp.ones((128, 128), BF16)) + EMPTY).astype(BF16).reshape(DP, SLOT, 128)
 
 
 def order_columns(w, wp):
@@ -125,7 +131,7 @@
 def step_kernel(
     texts_in, qkv_in, out_in, self_in, neigh_in, ids_in, cot_in,
     o_mixed, o_ngrad, o_sn, o_out,
-    mixed, ngrad, fin_sn, fin_out, tx, wq, wp, qkv, w_out, w_self, w_neigh, ids, cot, acc, tmean, pooled, want, gh, ght, cnt,
+    mixed, ngrad, fin_sn, fin_out, tx, wq, wp, qkv, w_out, w_self, w_neigh, ids, cot, acc, tmean, pooled, want, spots, gh, ght, cnt,
     asked, sel, sbufp, rbufp, sbuf, rbuf, sbuf2, rbuf2, sel_t, part, sums, cots, zsend, zall, full, e2, m2,
     emb_g, pool_g, agg_g, agp_g, dz2, dz_g, fact, fact_g, sn_s, sn_r, out_s, out_r,
     tsem, lsem, osem, ssem, rsem, z_s, z_r, y_s, y_r, c_s, c_r,
@@ -178,19 +184,19 @@
             later(dst.at[pl.ds(0, DP - 1)], phase)
 
     def to_mp(src, dst, phase):
-        for i in range(1, MP):
+        for i in MP_ORDER:
             to = (m + i) % MP
             send(src.at[to], dst.at[m], phase, d, to)
         dst[m] = src[m]
         later(dst.at[pl.ds(0, MP - 1)], phase)
 
     def share_mp(src, dst, phase):
-        for i in range(1, MP):
+        for i in MP_ORDER:
             send(src, dst.at[m], phase, d, (m + i) % MP)
         later(dst.at[pl.ds(0, MP - 1)], phase)
 
     def to_group(block, phase):
-        for i in range(1, NG):
+        for i in GROUP_ORDER:
             send(block.at[g], block.at[g], phase, z * NG + (g + i) % NG, m)
         later(block.at[pl.ds(0, NG - 1)], phase)
 
@@ -232,7 +238,7 @@
             sent(dst, phase)
 
     def scatter_z(src, dst, phase):
-        for i in range(1, NZ):
+        for i in FAR_FIRST[:-1]:
             to = (z + i) % NZ
             send(src.at[to], dst.at[z], phase, to * NG + g, m)
         dst[z] = src[z]
@@ -245,7 +251,7 @@
         )
 
     def along_y(fin, at, which):
-        for i in range(1, NY):
+        for i in MP_ORDER:
             pltpu.make_async_remote_copy(
                 src_ref=fin.at[g, at], dst_ref=fin.at[g, at], send_sem=y_s.at[which, i], recv_sem=y_r.at[which, i],
                 device_id=(z * NG + ((y + i) % NY) * 2 + c, m), device_id_type=MESH,
@@ -323,7 +329,7 @@
     lax.fori_loop(0, NG, greet, 0)
 
     names_in.wait()
-    routing(ids, want, gh, ght, cnt)
+    request_names(ids, want, spots)
     e2[...] = jnp.zeros_like(e2)
     m2[...] = jnp.zeros_like(m2)
     weight.wait()
@@ -340,7 +346,16 @@
         @pl.when(i == 0)
         def _():
             pl.semaphore_wait(bar, DP - 1 + MP - 1 + 2 * MP - is_diag.astype(jnp.int32))
-            to_dp(want, asked, ASK)
+            for k in FAR_FIRST:
+
+                def ask(j, none):
+                    to = ((z + k) % NZ) * NG + (g + j) % NG
+                    send(want.at[pl.ds(to, 1)], asked.at[pl.ds(d, 1)], ASK, to, m)
+                    return none
+
+                lax.fori_loop(1 if k == 0 else 0, NG, ask, 0)
+            asked[pl.ds(d, 1), :] = want[pl.ds(d, 1), :]
+
 
         return carry
 
@@ -367,12 +382,18 @@
     cots[m] = pad_rows(cot[...], PAD)
     share_mp(cots.at[m], cots, COT)
     got(asked.at[pl.ds(0, DP - 1)], ASK)
-    names = asked[...].reshape(DP * SLOT, 128).astype(F32)
-    hot = (names == iota((DP * SLOT, 128), 1).astype(F32)).astype(F32)
+    later(asked.at[pl.ds(0, DP - 1)], ASK)
+    row = iota((DP * SLOT, 1), 0)
+    block = (jnp.right_shift(row, 4) == iota((DP * SLOT, DP), 1)).astype(BF16)
+    lane = iota((DP * SLOT, 128), 1)
+    of_rank = jnp.where(lane == jnp.bitwise_and(row, 7), dot(block, asked[...].astype(BF16)), 0.0)
+    names = jnp.sum(of_rank, axis=1, keepdims=True) + (PAD / 8) * jnp.bitwise_and(row, 8).astype(F32)
+    hot = (names == lane.astype(F32)).astype(F32)
     sel[...] = hot.astype(BF16)
     halves(m2, pooled[...])
     sbufp[...] = rows_of(sel[...], m2[...])
     sel_t[...] = jnp.transpose(hot)[: 2 * PAD].astype(BF16)
+    routing(spots, gh, ght, cnt)
     got(sums.at[pl.ds(0, MP - 1)], POOL_SUM)
     embed = tmean[...] + (sums[0] + sums[1] + sums[2] + sums[3])
     embed = pad_rows(embed, PAD).astype(BF16)
@@ -412,7 +433,7 @@
     dz = (jnp.concatenate([cots[j] for j in range(MP)], axis=1).astype(F32) * slope).astype(BF16)
     for j in range(NG):
         dz2[j] = dz[:, j * 128 : j * 128 + 128]
-    for i in range(1, NG):
+    for i in GROUP_ORDER:
         to = (g + i) % NG
         send(dz2.at[to], dz_g.at[g], DZ_G, z * NG + to, m)
     dz_g[g] = dz2[g]
@@ -513,11 +534,12 @@
             f(NODE, COLS),
             f(NODE, COLS),
             b(PAD, COLS),
-            blocks,
+            f(DP, 128),
+            f(NODE, ids.shape[0]),
             b(2 * PAD, DP * SLOT),
             b(DP * SLOT, 128),
             f(PAD, COLS),
-            blocks,
+            f(DP, 128),
             b(DP * SLOT, 128),
             blocks,
             blocks,

time: 71.8 us -> 69.9 us (0.974)
  Pallas kernels: 71 us -> 69.1 us
    pallas_call x1, Pallas kernels: 68.1 us -> 66.2 us  [step(): pl.pallas_call(step_kernel, out_shape=[jax.ShapeDtypeStruct((NODE, COLS),...]
where the time goes in v5:
time: 69.9 us; the launch traced here: 69.8 us
  Pallas kernels  69.1 us (99%)
    pallas_call x1, Pallas kernels, step(): pl.pallas_call(step_kernel, out_shape=[jax.ShapeDtypeStruct((NODE, COLS),...  66.2 us
    pallas_call x1, Pallas kernels, finish(): pl.pallas_call(finish_kernel, out_shape=[jax.ShapeDtypeStruct((NODE, COLS...  2.96 us

profile of v5, /device:TPU:1, one launch (start us, length us, event | category | flops | bytes accessed | tf_op | source)
XLA Modules:
  0.0 69.8 jit_solution(12374922789255810305)
XLA Ops:
  0.6 66.2 %shard_map.110 = (bf16[24,256]{1,0:T(8,128)(2,1)}, bf16[24,256]{1,0:T(8,128)(2,1)}, bf16[8,8,2,32,128]{4,3,2,1,0:T(8,128)(2,1)}, bf16[8,8,32,128]{3,2,1,0:T(8,128)(2,1)}) custom-call(bf16[24,128,1024]{2,1,0:T(8,128)(2,1)} %texts_in.1, bf16[1024,768]{1,0:T(8,128)(2,1)} %qkv_in.1, bf16[256,1024]{1,0:T(8,128)(2,1)} %out_in.1, bf16[256,1024]{1,0:T(8,128)(2,1)} %self_in.1, ...), custom_call_target="tpu_custom_call" | custom-call | flops 7000000000 | bytes 12000000 | tf_op jit(solution)/shard_map/pallas_call | solution.py:510
  66.8 3.0 %shard_map.111 = (bf16[24,256]{1,0:T(8,128)(2,1)}, bf16[24,256]{1,0:T(8,128)(2,1)}, f32[256,1024]{1,0:T(8,128)}, f32[256,1024]{1,0:T(8,128)}, f32[256,1024]{1,0:T(8,128)}) custom-call(bf16[24,256]{1,0:T(8,128)(2,1)} %get-tuple-element.9.mixed, bf16[24,256]{1,0:T(8,128)(2,1)} %get-tuple-element.10.ngrad, bf16[8,8,2,32,128]{4,3,2,1,0:T(8,128)(2,1)} %get-tuple-element.11.sn, ...), custom_call_target="tpu_custom_call" | custom-call | bytes 5000000 | tf_op jit(solution)/shard_map/pallas_call | solution.py:623
